TPU v7x, 768 devices: a whole 4x8x12 slice. The times are simulated.
768 devices in a mesh: grp: 64 (over x, y, core), sub: 12 (over z).
Axes of the slice: x: 4, y: 8, z: 12, core: 2. Of those that a mesh axis runs over, the one named last changes fastest.
Arguments:
- tokens: bfloat16 [3072, 32, 256], P(('grp', 'sub')), may hold values from -64 to 64
- proj_weight: bfloat16 [256, 256], replicated, may hold values from -2 to 2
- match_grad: bfloat16 [98304, 1024], P(('grp', 'sub')), may hold values from -3072 to 3072
- edge_first: int32 [98304], P(('grp', 'sub')), may hold values from 0 to 47, as said below
- pair_second_image: int32 [98304], P(('grp', 'sub')), may hold values from 0 to 63, as said below
- send_pick: int32 [49152], P(('grp', 'sub')), may hold values from 0 to 3, as said below
Outputs:
- token_grad: bfloat16 [3072, 32, 256], P(('grp', 'sub'))
Inputs may be any that keep to these rules, and one draw needn't show every extreme that they name: On each device the pairs (edge_first, pair_second_image) are distinct. `pair_second_image`: on each device every receive slot 0 to 63 is named by at least one pair. `send_pick`: for each device and each index p of grp, the 1 entries of its send slots p * 1 to p + 1 - 1 name different images.
All inputs are finite; a program needn't handle non-finite values.
Results may differ from a plain program's by a relative error of at most 0.017.
Values may be sent and summed in bfloat16 or wider, within the bound.
A program may use at most 64 MiB of HBM per device.

v0:
```python
import jax
import jax.numpy as jnp
from jax import lax
from jax.sharding import PartitionSpec as P

EPSILON = 1e-05
SOFTMAX_COOLING = 0.1


def normalize(token_triple, proj_weight):
    image_count, length, feat_width = token_triple.shape
    feature = jnp.dot(
        token_triple.reshape(image_count * length, feat_width),
        proj_weight,
        preferred_element_type=jnp.float32,
    )
    inv_rms = lax.rsqrt(jnp.mean(feature * feature, axis=-1, keepdims=True) + EPSILON)
    normed = feature * inv_rms
    return (normed, inv_rms, normed.astype(jnp.bfloat16).reshape(image_count, length, feat_width))


def edge_terms(first_image_features, second_feats, match_block):
    score_scale = 1.0 / (first_image_features.shape[-1] * SOFTMAX_COOLING)
    scores = (
        jnp.einsum(
            "eid,ejd->eij", first_image_features, second_feats, preferred_element_type=jnp.float32
        )
        * score_scale
    )
    expo = jnp.exp(scores)
    rows = expo / jnp.sum(expo, axis=2, keepdims=True)
    cols = expo / jnp.sum(expo, axis=1, keepdims=True)
    incoming_gradient = match_block.astype(jnp.float32)
    d_rows = incoming_gradient * cols
    d_cols = incoming_gradient * rows
    d_scores = rows * (d_rows - jnp.sum(d_rows * rows, axis=2, keepdims=True)) + cols * (
        d_cols - jnp.sum(d_cols * cols, axis=1, keepdims=True)
    )
    d_scaled = (d_scores * score_scale).astype(jnp.bfloat16)
    grad_first = jnp.einsum(
        "eij,ejd->eid", d_scaled, second_feats, preferred_element_type=jnp.float32
    )
    grad_second = jnp.einsum(
        "eij,eid->ejd", d_scaled, first_image_features, preferred_element_type=jnp.float32
    )
    return (grad_first, grad_second)


def local(tokens, proj_weight, match_grad, edge_first, pair_second_image, send_pick):
    img_count, length, feat_width = tokens.shape
    normed, inv_rms, normed_b = normalize(tokens, proj_weight)
    raw_pool = lax.all_gather(tokens, "sub", axis=0, tiled=True)
    raw_received = lax.all_to_all(
        jnp.take(tokens, send_pick, axis=0), "grp", split_axis=0, concat_axis=0, tiled=True
    )
    pool = normalize(raw_pool, proj_weight)[2]
    received = normalize(raw_received, proj_weight)[2]
    pool_count = pool.shape[0]
    slot_count = received.shape[0]
    edge_count = edge_first.shape[0]
    grads = match_grad.reshape(edge_count, length, length)
    edge_block = 64

    def block_step(block_index, totals):
        pool_total, slot_total = totals
        block_start = block_index * edge_block
        first_images = lax.dynamic_slice_in_dim(edge_first, block_start, edge_block, 0)
        seconds = lax.dynamic_slice_in_dim(pair_second_image, block_start, edge_block, 0)
        block_grads = lax.dynamic_slice_in_dim(grads, block_start, edge_block, 0)
        grad_first, grad_second = edge_terms(
            jnp.take(pool, first_images, axis=0), jnp.take(received, seconds, axis=0), block_grads
        )
        pool_total = pool_total.at[first_images].add(grad_first)
        slot_total = slot_total.at[seconds].add(grad_second)
        return (pool_total, slot_total)

    start_totals = (
        jnp.zeros((pool_count, length, feat_width), jnp.float32),
        jnp.zeros((slot_count, length, feat_width), jnp.float32),
    )
    pool_total, slot_total = lax.fori_loop(0, edge_count // edge_block, block_step, start_totals)
    returned = lax.all_to_all(
        slot_total.astype(jnp.bfloat16), "grp", split_axis=0, concat_axis=0, tiled=True
    )
    owned = lax.psum_scatter(
        pool_total.astype(jnp.bfloat16), "sub", scatter_dimension=0, tiled=True
    ).astype(jnp.float32)
    pick_onehot = (jnp.arange(img_count, dtype=jnp.int32)[:, None] == send_pick[None, :]).astype(
        jnp.bfloat16
    )
    incoming_gradient = owned + jnp.einsum(
        "ir,rld->ild", pick_onehot, returned, preferred_element_type=jnp.float32
    )
    incoming_gradient = incoming_gradient.reshape(img_count * length, feat_width)
    feature_grad = (
        inv_rms
        * (
            incoming_gradient
            - normed * jnp.mean(incoming_gradient * normed, axis=-1, keepdims=True)
        )
    ).astype(jnp.bfloat16)
    token_grad = jnp.einsum(
        "nk,dk->nd", feature_grad, proj_weight, preferred_element_type=jnp.float32
    )
    return token_grad.astype(jnp.bfloat16).reshape(img_count, length, feat_width)


def solution(mesh):
    placed = (
        P(("grp", "sub"), None, None),
        P(),
        P(("grp", "sub"), None),
        P(("grp", "sub")),
        P(("grp", "sub")),
        P(("grp", "sub")),
    )
    return jax.shard_map(
        local, mesh=mesh, in_specs=placed, out_specs=P(("grp", "sub"), None, None), check_vma=False
    )
```

profile of v0, /device:TPU:2, one launch (start us, length us, event | category | flops | bytes accessed | tf_op | source)
XLA Modules:
  0.0 219.0 jit_solution(7112430921984724791)
XLA Ops:
  7.9 1.5 gather_fusion.2
  9.4 1.2 broadcast_select_fusion.6
  10.5 13.7 %all-to-all-start = ((bf16[64,32,256]{2,1,0:T(8,128)(2,1)}), bf16[64,32,256]{2,1,0:T(8,128)(2,1)S(1)}, u32[]{:S(2)}, u32[]{:S(2)}) async-start(bf16[64,32,256]{2,1,0:T(8,128)(2,1)} %broadcast_select_fusion.6), calls=%async_computation | async-start | bytes 2097152 | tf_op jit(solution)/shard_map/all_to_all | solution.py:53
  25.1 34.1 %all_gather.3 = bf16[48,32,256]{2,1,0:T(8,128)(2,1)S(1)} all-gather(bf16[4,32,256]{2,1,0:T(8,128)(2,1)S(1)} %copy-done.6), channel_id=1, replica_groups=mesh['grp'=64,'sub'=12] {'sub'}, dimensions={0}, use_global_device_ids=true | all-gather | bytes 851968 | tf_op jit(solution)/shard_map/all_gather | solution.py:52
  59.7 1.2 multiply_convert_fusion.1
  61.5 1.3 multiply_convert_fusion
  62.9 1.3 broadcast_in_dim.80
  64.2 1.6 broadcast_in_dim.81
  65.8 75.4 %while.15 = (s32[]{:T(128)}, f32[48,32,256]{2,1,0:T(8,128)}, f32[64,32,256]{2,1,0:T(8,128)}, s32[128]{0:T(128)S(1)}, bf16[48,32,256]{2,1,0:T(8,128)(2,1)}, /*ind...) while((s32[]{:T(128)}, f32[48,32,256]{2,1,0:T(8,128)}, ...), condition=%wide.region_10.11_spmd, body=%wide.region_3.10_spmd.sunk | while | flops 140456864 | bytes 41037088 | solution.py:81
  65.9 1.7 gather_fusion
  67.7 2.2 %gather_fusion.1 = bf16[64,32,256]{2,1,0:T(8,128)(2,1)S(1)} fusion(bf16[64,32,256]{2,1,0:T(8,128)(2,1)} %get-tuple-element.286, s32[1024]{0:T(1024)S(1)} %pad_clamp_fusion.6), kind=kCustom, calls=%fused_computation.1.clone.1 | custom fusion | bytes 2097408 | tf_op jit(solution)/shard_map/while/body/eval_jaxpr/jit(_take)/gather | solution.py:71
  71.0 1.7 fusion.59
  72.6 1.1 constant_dynamic-slice_fusion.2
  75.3 1.8 fusion.60
  77.2 4.2 %fusion.61 = f32[64,32,256]{2,1,0:T(8,128)S(1)} fusion(f32[64,32,32]{2,1,0:T(8,128)S(1)} %fusion.60, f32[64,32,32]{2,1,0:T(8,128)} %fusion.59, bf16[64,32,256]{2,1,0:T(8,128)(2,1)} %copy-done.3, pred[64]{0:T(512)(128)(4,1)S(1)} %get-tuple-element.255, f32[64,32,32]{2,1,0:T(8,128)} %copy-done.5, bf16[64,32,32]{2,1,0:T(8,128)(2,1)} %copy-done.4), kind=kOutput, calls=%fused_computation.29.clone.1 | convolution fusion | flops 34736160 | bytes 4063296 | tf_op jit(solution)/shard_map/while/body/eval_jaxpr/eij,ejd->eid/dot_general | solution.py:40
  81.4 9.0 %scatter_fusion = f32[48,32,256]{2,1,0:T(8,128)} fusion(f32[48,32,256]{2,1,0:T(8,128)} %get-tuple-element.269, s32[64]{0:T(128)S(1)} %get-tuple-element.252, f32[64,32,256]{2,1,0:T(8,128)S(1)} %fusion.61), kind=kCustom, calls=%fused_computation.3.clone.1 | custom fusion | flops 524288 | bytes 6291712 | tf_op jit(solution)/shard_map/while/body/eval_jaxpr/scatter-add | solution.py:73
  90.4 4.0 %fusion.62 = f32[64,32,256]{2,1,0:T(8,128)S(1)} fusion(f32[64,32,32]{2,1,0:T(8,128)S(1)} %fusion.60, f32[64,32,32]{2,1,0:T(8,128)} %fusion.59, bf16[64,32,256]{2,1,0:T(8,128)(2,1)} %copy-done.2, pred[64]{0:T(512)(128)(4,1)S(1)} %get-tuple-element.253, f32[64,32,32]{2,1,0:T(8,128)} %copy-done.5, bf16[64,32,32]{2,1,0:T(8,128)(2,1)} %copy-done.4), kind=kOutput, calls=%fused_computation.28.clone.1 | convolution fusion | flops 34736160 | bytes 4063296 | tf_op jit(solution)/shard_map/while/body/eval_jaxpr/eij,eid->ejd/dot_general | solution.py:43
  94.4 9.0 %scatter_fusion.1 = f32[64,32,256]{2,1,0:T(8,128)} fusion(f32[64,32,256]{2,1,0:T(8,128)} %get-tuple-element.270, s32[64]{0:T(128)S(1)} %get-tuple-element.254, f32[64,32,256]{2,1,0:T(8,128)S(1)} %fusion.62), kind=kCustom, calls=%fused_computation.4.clone.1 | custom fusion | flops 524288 | bytes 6291712 | tf_op jit(solution)/shard_map/while/body/eval_jaxpr/scatter-add | solution.py:74
  103.5 1.7 gather_fusion
  105.3 2.2 %gather_fusion.1 = bf16[64,32,256]{2,1,0:T(8,128)(2,1)S(1)} fusion(bf16[64,32,256]{2,1,0:T(8,128)(2,1)} %get-tuple-element.286, s32[1024]{0:T(1024)S(1)} %pad_clamp_fusion.6), kind=kCustom, calls=%fused_computation.1.clone.1 | custom fusion | bytes 2097408 | tf_op jit(solution)/shard_map/while/body/eval_jaxpr/jit(_take)/gather | solution.py:71
  108.6 1.7 fusion.59
  110.3 1.1 constant_dynamic-slice_fusion.2
  113.0 1.8 fusion.60
  114.8 4.2 %fusion.61 = f32[64,32,256]{2,1,0:T(8,128)S(1)} fusion(f32[64,32,32]{2,1,0:T(8,128)S(1)} %fusion.60, f32[64,32,32]{2,1,0:T(8,128)} %fusion.59, bf16[64,32,256]{2,1,0:T(8,128)(2,1)} %copy-done.3, pred[64]{0:T(512)(128)(4,1)S(1)} %get-tuple-element.255, f32[64,32,32]{2,1,0:T(8,128)} %copy-done.5, bf16[64,32,32]{2,1,0:T(8,128)(2,1)} %copy-done.4), kind=kOutput, calls=%fused_computation.29.clone.1 | convolution fusion | flops 34736160 | bytes 4063296 | tf_op jit(solution)/shard_map/while/body/eval_jaxpr/eij,ejd->eid/dot_general | solution.py:40
  119.0 9.0 %scatter_fusion = f32[48,32,256]{2,1,0:T(8,128)} fusion(f32[48,32,256]{2,1,0:T(8,128)} %get-tuple-element.269, s32[64]{0:T(128)S(1)} %get-tuple-element.252, f32[64,32,256]{2,1,0:T(8,128)S(1)} %fusion.61), kind=kCustom, calls=%fused_computation.3.clone.1 | custom fusion | flops 524288 | bytes 6291712 | tf_op jit(solution)/shard_map/while/body/eval_jaxpr/scatter-add | solution.py:73
  128.1 4.0 %fusion.62 = f32[64,32,256]{2,1,0:T(8,128)S(1)} fusion(f32[64,32,32]{2,1,0:T(8,128)S(1)} %fusion.60, f32[64,32,32]{2,1,0:T(8,128)} %fusion.59, bf16[64,32,256]{2,1,0:T(8,128)(2,1)} %copy-done.2, pred[64]{0:T(512)(128)(4,1)S(1)} %get-tuple-element.253, f32[64,32,32]{2,1,0:T(8,128)} %copy-done.5, bf16[64,32,32]{2,1,0:T(8,128)(2,1)} %copy-done.4), kind=kOutput, calls=%fused_computation.28.clone.1 | convolution fusion | flops 34736160 | bytes 4063296 | tf_op jit(solution)/shard_map/while/body/eval_jaxpr/eij,eid->ejd/dot_general | solution.py:43
  132.1 9.1 %scatter_fusion.1 = f32[64,32,256]{2,1,0:T(8,128)} fusion(f32[64,32,256]{2,1,0:T(8,128)} %get-tuple-element.270, s32[64]{0:T(128)S(1)} %get-tuple-element.254, f32[64,32,256]{2,1,0:T(8,128)S(1)} %fusion.62), kind=kCustom, calls=%fused_computation.4.clone.1 | custom fusion | flops 524288 | bytes 6291712 | tf_op jit(solution)/shard_map/while/body/eval_jaxpr/scatter-add | solution.py:74
  141.2 2.8 %convert_element_type.40 = bf16[64,32,256]{2,1,0:T(8,128)(2,1)} convert(f32[64,32,256]{2,1,0:T(8,128)} %get-tuple-element.146) | non-fusion elementwise | flops 524288 | bytes 3145728 | tf_op jit(solution)/shard_map/convert_element_type | solution.py:83
  144.0 10.5 %all-to-all-start.1 = ((bf16[64,32,256]{2,1,0:T(8,128)(2,1)}), bf16[64,32,256]{2,1,0:T(8,128)(2,1)S(1)}, u32[]{:S(2)}, u32[]{:S(2)}) async-start(bf16[64,32,256]{2,1,0:T(8,128)(2,1)} %convert_element_type.40), calls=%async_computation.2 | async-start | bytes 2097152 | tf_op jit(solution)/shard_map/all_to_all | solution.py:82
  154.6 1.0 convert_element_type.38
  155.9 25.8 %all-to-all-done.1 = bf16[64,32,256]{2,1,0:T(8,128)(2,1)S(1)} async-done(((bf16[64,32,256]{2,1,0:T(8,128)(2,1)}), bf16[64,32,256]{2,1,0:T(8,128)(2,1)S(1)}, u32[]{:S(2)}, u32[]{:S(2)}) %all-to-all-start.1) | async-done | bytes 1048608 | tf_op jit(solution)/shard_map/all_to_all | solution.py:82
  182.3 27.8 %reduce-scatter.2.cloned.1.call-done = bf16[4,32,256]{2,1,0:T(8,128)(2,1)} async-done(((bf16[48,32,256]{2,1,0:T(8,128)(2,1)}), bf16[4,32,256]{2,1,0:T(8,128)(2,1)}) %reduce-scatter.2.cloned.1.call-update) | async-done | bytes 65552 | tf_op jit(solution)/shard_map/reduce_scatter | solution.py:85
  (59 shorter events, 11.7 us)
Async XLA Ops:
  6.5 52.7 %copy-start = (bf16[256,256]{1,0:T(8,128)(2,1)S(1)}, bf16[256,256]{1,0:T(8,128)(2,1)}, u32[]{:S(2)}) copy-start(bf16[256,256]{1,0:T(8,128)(2,1)} %param.9) | copy-start | bytes 393220
  9.4 14.9 %copy-start.7 = (bf16[128,1024]{1,0:T(8,128)(2,1)S(1)}, bf16[128,1024]{1,0:T(8,128)(2,1)}, u32[]{:S(2)}) copy-start(bf16[128,1024]{1,0:T(8,128)(2,1)} %param.10) | copy-start | bytes 786436
  9.4 15.8 %copy-start.6 = (bf16[4,32,256]{2,1,0:T(8,128)(2,1)S(1)}, bf16[4,32,256]{2,1,0:T(8,128)(2,1)}, u32[]{:S(2)}) copy-start(bf16[4,32,256]{2,1,0:T(8,128)(2,1)} %param.8) | copy-start | bytes 196612
  10.5 50.5 %all-to-all-start = ((bf16[64,32,256]{2,1,0:T(8,128)(2,1)}), bf16[64,32,256]{2,1,0:T(8,128)(2,1)S(1)}, u32[]{:S(2)}, u32[]{:S(2)}) async-start(bf16[64,32,256]{2,1,0:T(8,128)(2,1)} %broadcast_select_fusion.6), calls=%async_computation | async-start | bytes 2097152 | tf_op jit(solution)/shard_map/all_to_all | solution.py:53
  62.9 3.0 %copy-start.8 = (s32[128]{0:T(128)S(1)}, s32[128]{0:T(128)}, u32[]{:S(2)}) copy-start(s32[128]{0:T(128)} %param.11) | copy-start | bytes 1540
  62.9 3.0 %copy-start.9 = (s32[128]{0:T(128)S(1)}, s32[128]{0:T(128)}, u32[]{:S(2)}) copy-start(s32[128]{0:T(128)} %param.12) | copy-start | bytes 1540
  67.7 3.1 %copy-start.2 = (bf16[64,32,256]{2,1,0:T(8,128)(2,1)}, bf16[64,32,256]{2,1,0:T(8,128)(2,1)S(1)}, u32[]{:S(2)}) copy-start(bf16[64,32,256]{2,1,0:T(8,128)(2,1)S(1)} %gather_fusion) | copy-start | bytes 3145732 | tf_op jit(solution)/shard_map/while
  69.9 1.1 copy-start.3
  71.0 3.5 %copy-start.5 = (f32[64,32,32]{2,1,0:T(8,128)}, f32[64,32,32]{2,1,0:T(8,128)S(1)}, u32[]{:S(2)}) copy-start(f32[64,32,32]{2,1,0:T(8,128)S(1)} %fusion.58) | copy-start | bytes 786436 | tf_op jit(solution)/shard_map/while
  74.5 0.8 copy-start.4
  105.3 3.1 %copy-start.2 = (bf16[64,32,256]{2,1,0:T(8,128)(2,1)}, bf16[64,32,256]{2,1,0:T(8,128)(2,1)S(1)}, u32[]{:S(2)}) copy-start(bf16[64,32,256]{2,1,0:T(8,128)(2,1)S(1)} %gather_fusion) | copy-start | bytes 3145732 | tf_op jit(solution)/shard_map/while
  107.5 1.1 copy-start.3
  108.6 3.5 %copy-start.5 = (f32[64,32,32]{2,1,0:T(8,128)}, f32[64,32,32]{2,1,0:T(8,128)S(1)}, u32[]{:S(2)}) copy-start(f32[64,32,32]{2,1,0:T(8,128)S(1)} %fusion.58) | copy-start | bytes 786436 | tf_op jit(solution)/shard_map/while
  112.2 0.8 copy-start.4
  141.2 13.4 %copy-start.1 = (f32[48,32,256]{2,1,0:T(8,128)S(1)}, f32[48,32,256]{2,1,0:T(8,128)}, u32[]{:S(2)}) copy-start(f32[48,32,256]{2,1,0:T(8,128)} %get-tuple-element.145) | copy-start | bytes 4718596
  144.0 37.7 %all-to-all-start.1 = ((bf16[64,32,256]{2,1,0:T(8,128)(2,1)}), bf16[64,32,256]{2,1,0:T(8,128)(2,1)S(1)}, u32[]{:S(2)}, u32[]{:S(2)}) async-start(bf16[64,32,256]{2,1,0:T(8,128)(2,1)} %convert_element_type.40), calls=%async_computation.2 | async-start | bytes 2097152 | tf_op jit(solution)/shard_map/all_to_all | solution.py:82
  154.5 27.1 %copy-start.10 = (s32[64]{0:T(128)S(1)}, s32[64]{0:T(128)}, u32[]{:S(2)}) copy-start(s32[64]{0:T(128)} %param.13) | copy-start | bytes 772
  154.6 55.5 %reduce-scatter.2.cloned.1.call-start = ((), (), s32[]{:S(2)}) async-start(), calls=%async_computation.3 | async-start | bytes 851968 | tf_op jit(solution)/shard_map/reduce_scatter | solution.py:85
Sparse Core Ops, SparseCore 0:
  158.5 51.5 reduce-scatter.1
where the time goes:
time: 221 us; the launch traced here: 219 us
  waiting for transfers between devices  53.5 us (24%)
  other arithmetic  50.1 us (23%)
  blocking collectives  34.1 us (15%)
  starting transfers between devices  24.3 us (11%)
  matrix products  24.3 us (11%)
  local copies, waits for them, and re-layouts  18.9 us (9%)
  between operations  13.5 us (6%)
    all_gather x1, blocking collectives, local(): raw_pool = lax.all_gather(tokens, 'sub', axis=0, tiled=True)  34.1 us
    reduce_scatter x1, waiting for transfers between devices, local(): lax.psum_scatter(pool_total.astype(jnp.bfloat16), 'sub', scatter_dimensio...  27.8 us
    all_to_all x1, waiting for transfers between devices, local(): lax.all_to_all(slot_total.astype(jnp.bfloat16), 'grp', split_axis=0, conc...  25.8 us
    scatter-add x2, other arithmetic, block_step(): slot_total = slot_total.at[seconds].add(grad_second)  18.1 us
    scatter-add x2, other arithmetic, block_step(): pool_total = pool_total.at[first_images].add(grad_first)  18 us
    all_to_all x1, starting transfers between devices, local(): lax.all_to_all(jnp.take(tokens, send_pick, axis=0), 'grp', split_axis=0,...  13.7 us
    all_to_all x1, starting transfers between devices, local(): lax.all_to_all(slot_total.astype(jnp.bfloat16), 'grp', split_axis=0, conc...  10.5 us
    dot_general x2, matrix products, edge_terms(): jnp.einsum('eij,ejd->eid', d_scaled, second_feats, preferred_element_type...  8.5 us
  transfers between devices with their start and end apart: 3, of which 2 were waited for; matrix products, arithmetic and copies ran while one was open for 2% of the time, Pallas kernels for 0%

commit v1 on v0

v1 whole, which is shorter than its diff:
```python
import functools

import jax
import jax.numpy as jnp
from jax import lax
from jax.experimental import pallas as pl
from jax.experimental.pallas import tpu as pltpu
from jax.sharding import PartitionSpec as P

EPSILON = 1e-05
SOFTMAX_COOLING = 0.1
MESH = pl.DeviceIdType.MESH
LANES = 128
VMEM_LIMIT = 40 * 1024 * 1024
GRID = (4, 8, 2)


def place_of(offset, ring):
    offset %= ring
    return 0 if offset == 0 else 2 * offset - 1 if 2 * offset <= ring else 2 * (ring - offset)


class Where:
    def __init__(self, grid, ring_z):
        _, self.ring_y, cores = grid
        self.cores, self.ring_z, self.peers = cores, ring_z, grid[0] * cores
        grp = lax.axis_index("grp")
        self.z = lax.axis_index("sub")
        self.y = lax.rem(lax.div(grp, cores), self.ring_y)
        self.s = lax.div(grp, cores * self.ring_y) * cores + lax.rem(grp, cores)

    def group(self, s, y):
        return (lax.div(s, self.cores) * self.ring_y + y) * self.cores + lax.rem(s, self.cores)

    def along_y(self, step):
        return {"grp": self.group(self.s, lax.rem(self.y + step + self.ring_y, self.ring_y))}

    def z_at(self, step):
        return lax.rem(self.z + step + self.ring_z, self.ring_z)

    def along_z(self, step):
        return {"sub": self.z_at(step)}

    def s_at(self, turn):
        return lax.rem(self.s + turn, self.peers)

    def across(self, turn):
        return {"grp": self.group(self.s_at(turn), self.y)}

    def greet(self):
        barrier = pltpu.get_barrier_semaphore()
        others = [self.along_y(1), self.along_y(-1), self.along_z(1), self.along_z(-1)]
        others += [self.across(turn) for turn in range(1, self.peers)]
        for other in others:
            pl.semaphore_signal(barrier, inc=1, device_id=other, device_id_type=MESH)
        return lambda: pl.semaphore_wait(barrier, len(others))


def send(src, dst, send_sem, recv_sem, device):
    copy = pltpu.make_async_remote_copy(
        src_ref=src,
        dst_ref=dst,
        send_sem=send_sem,
        recv_sem=recv_sem,
        device_id=device,
        device_id_type=MESH,
    )
    copy.start()
    return copy


def batches(ring):
    half = ring // 2
    return [(0, 1)] + [(2 * d - 1, 2) for d in range(1, half)] + [(ring - 1, 1)]


def rows_at(index, count):
    return pl.ds(pl.multiple_of(index * count, count), count)


def chooser(pick_row, images, length):
    shape = (images * length, pick_row.shape[1])
    row = lax.broadcasted_iota(jnp.int32, shape, 0)
    column = lax.broadcasted_iota(jnp.int32, shape, 1)
    image = lax.div(row, length).astype(jnp.float32)
    same = lax.rem(row, length) == lax.rem(column, length)
    return jnp.where(same & (image == pick_row), 1.0, 0.0).astype(jnp.bfloat16)


def gather_kernel(
    grid,
    ring_z,
    images,
    length,
    picks,
    tokens,
    weight,
    grads,
    seconds,
    pool,
    received,
    laid,
    places,
    pick_rows,
    feature,
    blocks,
    stage,
    y_send,
    y_recv,
    z_send,
    z_recv,
    x_send,
    x_recv,
):
    here = Where(grid, ring_z)
    ring_y, peers = here.ring_y, here.peers
    rows, width = tokens.shape
    block_rows = blocks.shape[1]
    met = here.greet()

    projected = jnp.dot(tokens[...], weight[...], preferred_element_type=jnp.float32)
    feature[...] = projected
    mean_square = jnp.mean(projected * projected, axis=-1, keepdims=True)
    normed = (projected * lax.rsqrt(mean_square + EPSILON)).astype(jnp.bfloat16)
    blocks[0, :rows] = normed
    pool[here.z] = normed
    tail = (block_rows - rows, peers * length)
    tail_row = lax.broadcasted_iota(jnp.int32, tail, 0)
    tail_peer = lax.div(lax.broadcasted_iota(jnp.int32, tail, 1), length)
    table = jnp.zeros(tail, jnp.int32)
    for y in range(ring_y):
        for s in range(peers):
            slot = (s // here.cores * ring_y + y) * here.cores + s % here.cores
            table = jnp.where((tail_row == y) & (tail_peer == s), picks[slot], table)
    blocks[0, rows:] = table.astype(jnp.float32).astype(jnp.bfloat16)
    met()

    half_y, half_z = ring_y // 2, ring_z // 2
    y_copies, z_copies, x_copies = [], [], []

    def forward_y(step):
        for way, turn in enumerate((1, -1)):
            part = slice(0, block_rows)
            if step == half_y:
                part = slice(0, rows // 2) if way == 0 else slice(rows // 2, block_rows)
            part = pl.ds(part.start, part.stop - part.start)
            y_copies.append(
                send(
                    blocks.at[place_of(-turn * (step - 1), ring_y), part],
                    blocks.at[place_of(-turn * step, ring_y), part],
                    y_send.at[way, step - 1],
                    y_recv.at[way, step - 1],
                    here.along_y(turn),
                )
            )

    def forward_z(step):
        for way, turn in enumerate((1, -1)):
            part = pl.ds(0, rows) if step < half_z else pl.ds(way * (rows // 2), rows // 2)
            owner = here.z_at(-turn * (step - 1))
            z_copies.append(
                send(
                    pool.at[owner, part],
                    pool.at[owner, part],
                    z_send.at[way, step - 1],
                    z_recv.at[way, step - 1],
                    here.along_z(turn),
                )
            )

    own = rows_at(here.s, length)

    def choose(batch, place, count):
        for at in range(place, place + count):
            rows_of_y = blocks[at, rows:].astype(jnp.float32)
            mine = jnp.sum(jnp.where(tail_row == here.y, rows_of_y, 0.0), axis=0, keepdims=True)
            pick_rows[at] = jnp.broadcast_to(mine, pick_rows.shape[1:])
            stage[at] = lax.dot_general(
                chooser(mine, images, length),
                blocks[at, :rows],
                (((0,), (0,)), ((), ())),
                preferred_element_type=jnp.float32,
            ).astype(jnp.bfloat16)
        for turn in range(1, peers):
            x_copies.append(
                send(
                    stage.at[pl.ds(place, count), rows_at(here.s_at(turn), length)],
                    received.at[pl.ds(place, count), own],
                    x_send.at[batch, turn - 1],
                    x_recv.at[batch, turn - 1],
                    here.across(turn),
                )
            )
        for at in range(place, place + count):
            received[at, own] = stage[at, own]

    forward_y(1)
    forward_z(1)
    plan = batches(ring_y)
    choose(0, *plan[0])

    slot = seconds[...]
    offset = lax.rem(lax.rem(lax.div(slot, here.cores), ring_y) - here.y + ring_y, ring_y)
    near = jnp.where(2 * offset <= ring_y, 2 * offset - 1, 2 * (ring_y - offset))
    place = jnp.where(offset == 0, 0, near)
    peer = lax.div(slot, here.cores * ring_y) * here.cores + lax.rem(slot, here.cores)
    places[...] = place * peers + peer

    across = LANES // length
    groups = grads.shape[0] // across
    lane_block = lax.div(lax.broadcasted_iota(jnp.int32, (groups, LANES), 1), length)

    def lay(tile):
        wide = grads[:, tile * LANES : (tile + 1) * LANES].astype(jnp.float32)
        parts = [wide[q * groups : (q + 1) * groups] for q in range(across)]
        for r in range(across):
            total = None
            for q in range(across):
                shift = (q - r) % across * length
                moved = pltpu.roll(parts[q], shift, 1) if shift else parts[q]
                total = moved if total is None else jnp.where(lane_block == q, moved, total)
            i = tile * across + r
            laid[i * groups : (i + 1) * groups] = total

    tiles = grads.shape[1] // LANES
    todo = list(range(tiles))
    for step in range(1, max(half_y, half_z) + 1):
        if todo:
            lay(todo.pop(0))
        if step <= half_y:
            for copy in y_copies[2 * step - 2 : 2 * step]:
                copy.wait_recv()
            if step < half_y:
                forward_y(step + 1)
        if step <= half_z:
            for copy in z_copies[2 * step - 2 : 2 * step]:
                copy.wait_recv()
            if step < half_z:
                forward_z(step + 1)
        if step <= half_y:
            choose(step, *plan[step])
    for tile in todo:
        lay(tile)
    for copy in x_copies:
        copy.wait_recv()
    for copy in y_copies + z_copies + x_copies:
        copy.wait_send()


def pair_kernel(
    length,
    first_ref,
    place_ref,
    pool,
    received,
    laid,
    pool_part,
    slot_part,
    pool_total,
    slot_total,
):
    pairs = first_ref.shape[1]
    across = LANES // length
    groups = pairs // across
    width = pool.shape[1]
    scale = 1.0 / (width * SOFTMAX_COOLING)
    together = 4

    pool_total[...] = jnp.zeros_like(pool_total)
    slot_total[...] = jnp.zeros_like(slot_total)
    side = (LANES, LANES)
    row_block = lax.div(lax.broadcasted_iota(jnp.int32, side, 0), length)
    lane_block = lax.div(lax.broadcasted_iota(jnp.int32, side, 1), length)
    diagonal = row_block == lane_block
    ones = jnp.where(diagonal, 1.0, 0.0).astype(jnp.bfloat16)
    ones = jnp.concatenate([ones, ones], axis=0)
    narrow = lax.div(lax.broadcasted_iota(jnp.int32, (length, LANES), 1), length)

    def block_sums(values):
        high = values.astype(jnp.bfloat16)
        low = (values - high.astype(jnp.float32)).astype(jnp.bfloat16)
        return jnp.dot(
            jnp.concatenate([high, low], axis=1), ones, preferred_element_type=jnp.float32
        )

    def step(chunk, carry):
        firsts, seconds, f_at, s_at, scores, incoming = [], [], [], [], [], []
        for n in range(together):
            g = chunk * together + n
            f_at.append([rows_at(first_ref[0, q * groups + g], length) for q in range(across)])
            s_at.append([rows_at(place_ref[0, q * groups + g], length) for q in range(across)])
            firsts.append(jnp.concatenate([pool[at] for at in f_at[n]], axis=0))
            seconds.append(jnp.concatenate([received[at] for at in s_at[n]], axis=0))
            full = lax.dot_general(
                firsts[n],
                seconds[n],
                (((1,), (1,)), ((), ())),
                preferred_element_type=jnp.float32,
            )
            packed = full[:length]
            for q in range(1, across):
                packed = jnp.where(narrow == q, full[q * length : (q + 1) * length], packed)
            scores.append(packed)
            incoming.append(laid[pl.ds(g, length, stride=groups), :])
        shape = (together, length, LANES)
        expo = jnp.exp(jnp.concatenate(scores, axis=0) * scale)
        gradient = jnp.concatenate(incoming, axis=0)
        rows = expo / block_sums(expo)
        expo = expo.reshape(shape)
        cols = (expo / jnp.sum(expo, axis=1, keepdims=True)).reshape(rows.shape)
        both = gradient * rows * cols
        over_second = block_sums(both)
        over_first = jnp.sum(both.reshape(shape), axis=1, keepdims=True)
        part = (cols.reshape(shape) * over_first).reshape(rows.shape)
        d_scaled = ((2.0 * both - rows * over_second - part) * scale).astype(jnp.bfloat16)
        for n in range(together):
            mine = d_scaled[n * length : (n + 1) * length]
            wide = jnp.concatenate([mine] * across, axis=0)
            wide = jnp.where(diagonal, wide, jnp.zeros_like(wide))
            grad_first = jnp.dot(wide, seconds[n], preferred_element_type=jnp.float32)
            grad_second = lax.dot_general(
                wide, firsts[n], (((0,), (0,)), ((), ())), preferred_element_type=jnp.float32
            )
            for q in range(across):
                part = slice(q * length, (q + 1) * length)
                pool_total[f_at[n][q]] += grad_first[part]
                slot_total[s_at[n][q]] += grad_second[part]
        return carry

    lax.fori_loop(0, groups // together, step, 0)
    pool_part[...] = pool_total[...].astype(jnp.bfloat16)
    slot_part[...] = slot_total[...].astype(jnp.bfloat16)


def return_kernel(
    grid,
    ring_z,
    images,
    length,
    slots,
    pool,
    pick_rows,
    feature,
    feature_grad,
    arrived,
    choosers,
    y_in,
    y_out,
    z_in,
    z_out,
    y_send,
    y_recv,
    z_send,
    z_recv,
    x_send,
    x_recv,
):
    here = Where(grid, ring_z)
    ring_y, peers = here.ring_y, here.peers
    rows, width = feature.shape
    half_y, half_z = ring_y // 2, ring_z // 2
    met = here.greet()
    own = rows_at(here.s, length)
    plan = batches(ring_y)
    met()

    y_copies, z_copies, x_copies = [], [], {}

    def ring_z_send(step, source_of):
        for way, turn in enumerate((1, -1)):
            part = pl.ds(way * (rows // 2), rows // 2) if step == 1 else pl.ds(0, rows)
            z_copies.append(
                send(
                    source_of(way, turn).at[part],
                    z_in.at[way, step - 1, part],
                    z_send.at[way, step - 1],
                    z_recv.at[way, step - 1],
                    here.along_z(turn),
                )
            )

    def ring_y_send(step):
        for way, turn in enumerate((1, -1)):
            part = pl.ds(way * (rows // 2), rows // 2) if step == 1 else pl.ds(0, rows)
            y_copies.append(
                send(
                    y_out.at[way, step - 1, part],
                    y_in.at[way, step - 1, part],
                    y_send.at[way, step - 1],
                    y_recv.at[way, step - 1],
                    here.along_y(turn),
                )
            )

    ring_z_send(1, lambda way, turn: pool.at[here.z_at(turn * half_z)])
    for distance in range(half_y, -1, -1):
        place, count = plan[distance]
        x_copies[distance] = [
            send(
                slots.at[pl.ds(place, count), rows_at(here.s_at(turn), length)],
                arrived.at[pl.ds(place, count), own],
                x_send.at[distance, turn - 1],
                x_recv.at[distance, turn - 1],
                here.across(turn),
            )
            for turn in range(1, peers)
        ]
    for at in range(ring_y):
        arrived[at, own] = slots[at, own]
        choosers[at] = chooser(pick_rows[at, :1], images, length)

    def summed(place):
        return jnp.dot(choosers[place], arrived[place], preferred_element_type=jnp.float32)

    def wait_x(distance):
        for copy in x_copies[distance]:
            copy.wait_recv()

    def joined(total, ins, way, step):
        if step > 1:
            return total + ins[way, step - 1].astype(jnp.float32)
        low = way * (rows // 2)
        added = total[low : low + rows // 2] + ins[way, 0, low : low + rows // 2].astype(jnp.float32)
        rest = total[rows // 2 :] if way == 0 else total[: rows // 2]
        return jnp.concatenate([added, rest] if way == 0 else [rest, added], axis=0)

    for step in range(1, max(half_y, half_z) + 1):
        if 1 < step <= half_z:
            for copy in z_copies[2 * step - 4 : 2 * step - 2]:
                copy.wait_recv()
            for way, turn in enumerate((1, -1)):
                mine = pool[here.z_at(turn * (half_z - step + 1))].astype(jnp.float32)
                z_out[way, step - 1] = joined(mine, z_in, way, step - 1).astype(jnp.bfloat16)
            ring_z_send(step, lambda way, turn: z_out.at[way, step - 1])
        if step <= half_y:
            distance = half_y - step + 1
            wait_x(distance)
            if step == 1:
                total = summed(ring_y - 1)
                for way in range(2):
                    y_out[way, 0] = total.astype(jnp.bfloat16)
            else:
                totals = [summed(place_of(turn * distance, ring_y)) for turn in (1, -1)]
                for copy in y_copies[2 * step - 4 : 2 * step - 2]:
                    copy.wait_recv()
                for way in range(2):
                    y_out[way, step - 1] = joined(totals[way], y_in, way, step - 1).astype(
                        jnp.bfloat16
                    )
            ring_y_send(step)
    wait_x(0)
    gradient = summed(0) + pool[here.z].astype(jnp.float32)
    projected = feature[...]
    mean_square = jnp.mean(projected * projected, axis=-1, keepdims=True)
    inv_rms = lax.rsqrt(mean_square + EPSILON)
    normed = projected * inv_rms
    for copy in y_copies[2 * half_y - 2 :] + z_copies[2 * half_z - 2 :]:
        copy.wait_recv()
    for way in range(2):
        gradient = joined(gradient, y_in, way, half_y)
        gradient = joined(gradient, z_in, way, half_z)
    mean = jnp.mean(gradient * normed, axis=-1, keepdims=True)
    feature_grad[...] = (inv_rms * (gradient - normed * mean)).astype(jnp.bfloat16)
    for copy in y_copies + z_copies + sum(x_copies.values(), []):
        copy.wait_send()


def in_vmem(count):
    return [pl.BlockSpec(memory_space=pltpu.VMEM)] * count


def in_smem(count):
    return [pl.BlockSpec(memory_space=pltpu.SMEM)] * count


def ring_semaphores(half_y, half_z, peers):
    dma = pltpu.SemaphoreType.DMA
    pairs = [(2, half_y), (2, half_z), (half_y + 1, peers - 1)]
    return [dma(shape) for shape in pairs for _ in range(2)]


def local(grid, ring_z, tokens, proj_weight, match_grad, edge_first, pair_second_image, send_pick):
    images, length, width = tokens.shape
    rows = images * length
    pairs = edge_first.shape[0]
    ring_y, peers = grid[1], grid[0] * grid[2]
    half_y, half_z = ring_y // 2, ring_z // 2
    bf16, f32 = jnp.bfloat16, jnp.float32
    shape = jax.ShapeDtypeStruct

    pool, received, laid, places, pick_rows, feature = pl.pallas_call(
        functools.partial(gather_kernel, grid, ring_z, images, length),
        out_shape=(
            shape((ring_z, rows, width), bf16),
            shape((ring_y, peers * length, width), bf16),
            shape((pairs * length * length // LANES, LANES), f32),
            shape((1, pairs), jnp.int32),
            shape((ring_y, 8, peers * length), f32),
            shape((rows, width), f32),
        ),
        in_specs=in_smem(1) + in_vmem(4),
        out_specs=tuple(in_vmem(6)),
        scratch_shapes=[
            pltpu.VMEM((ring_y, rows + 16, width), bf16),
            pltpu.VMEM((ring_y, peers * length, width), bf16),
            *ring_semaphores(half_y, half_z, peers),
        ],
        compiler_params=pltpu.CompilerParams(
            collective_id=0, has_side_effects=True, vmem_limit_bytes=VMEM_LIMIT
        ),
        name="gather_images",
    )(
        send_pick,
        tokens.reshape(rows, width),
        proj_weight,
        match_grad,
        pair_second_image.reshape(1, pairs),
    )

    pool_part, slot_part = pl.pallas_call(
        functools.partial(pair_kernel, length),
        out_shape=(
            shape((ring_z * rows, width), bf16),
            shape((ring_y * peers * length, width), bf16),
        ),
        in_specs=in_smem(2) + in_vmem(3),
        out_specs=tuple(in_vmem(2)),
        scratch_shapes=[
            pltpu.VMEM((ring_z * rows, width), f32),
            pltpu.VMEM((ring_y * peers * length, width), f32),
        ],
        compiler_params=pltpu.CompilerParams(vmem_limit_bytes=VMEM_LIMIT),
        name="pair_gradients",
    )(
        edge_first.reshape(1, pairs),
        places,
        pool.reshape(ring_z * rows, width),
        received.reshape(ring_y * peers * length, width),
        laid,
    )

    feature_grad = pl.pallas_call(
        functools.partial(return_kernel, grid, ring_z, images, length),
        out_shape=shape((rows, width), bf16),
        in_specs=in_vmem(4),
        out_specs=pl.BlockSpec(memory_space=pltpu.VMEM),
        scratch_shapes=[
            pltpu.VMEM((ring_y, peers * length, width), bf16),
            pltpu.VMEM((ring_y, rows, peers * length), bf16),
            pltpu.VMEM((2, half_y, rows, width), bf16),
            pltpu.VMEM((2, half_y, rows, width), bf16),
            pltpu.VMEM((2, half_z, rows, width), bf16),
            pltpu.VMEM((2, half_z, rows, width), bf16),
            *ring_semaphores(half_y, half_z, peers),
        ],
        compiler_params=pltpu.CompilerParams(
            collective_id=1, has_side_effects=True, vmem_limit_bytes=VMEM_LIMIT
        ),
        name="return_gradients",
    )(
        slot_part.reshape(ring_y, peers * length, width),
        pool_part.reshape(ring_z, rows, width),
        pick_rows,
        feature,
    )
    token_grad = lax.dot_general(
        feature_grad, proj_weight, (((1,), (1,)), ((), ())), preferred_element_type=f32
    )
    return token_grad.astype(bf16).reshape(images, length, width)


def solution(mesh, grid=GRID):
    placed = (
        P(("grp", "sub"), None, None),
        P(),
        P(("grp", "sub"), None),
        P(("grp", "sub")),
        P(("grp", "sub")),
        P(("grp", "sub")),
    )
    return jax.shard_map(
        functools.partial(local, grid, mesh.shape["sub"]),
        mesh=mesh,
        in_specs=placed,
        out_specs=P(("grp", "sub"), None, None),
        check_vma=False,
    )
```

time: 221 us -> 82.4 us (0.37)
  the two profiles are of different devices: /device:TPU:2 before, /device:TPU:16 now
where the time goes in v1:
time: 82.4 us; the launch traced here: 82.1 us
  Pallas kernels  77.2 us (94%)
  local copies, waits for them, and re-layouts  4.02 us (5%)
  matrix products  0.83 us (1%)
    pallas_call x1, Pallas kernels, local(): pl.pallas_call(functools.partial(gather_kernel, grid, ring_z, images, len...  40.2 us
    pallas_call x1, Pallas kernels, local(): pl.pallas_call(functools.partial(return_kernel, grid, ring_z, images, len...  29.8 us
    pallas_call x1, Pallas kernels, local(): pl.pallas_call(functools.partial(pair_kernel, length), out_shape=(shape((...  7.15 us
    unnamed x14, local copies, waits for them, and re-layouts  4.02 us

profile of v1, /device:TPU:16, one launch (start us, length us, event | category | flops | bytes accessed | tf_op | source)
XLA Modules:
  0.0 82.1 jit_solution(7853999704534277672)
XLA Ops:
  0.0 0.0 copy-start.4
  0.0 0.0 copy-start.5
  0.0 0.7 copy-done.4
  0.7 0.0 copy-done.5
  0.7 0.0 copy-start
  0.7 0.9 %copy-done = bf16[256,256]{1,0:T(8,128)(2,1)S(1)} copy-done((bf16[256,256]{1,0:T(8,128)(2,1)S(1)}, bf16[256,256]{1,0:T(8,128)(2,1)}, u32[]{:S(2)}) %copy-start) | copy-done | bytes 131096
  1.6 0.0 copy-start.2
  1.6 0.9 %copy-done.2 = bf16[128,1024]{1,0:T(8,128)(2,1)S(1)} copy-done((bf16[128,1024]{1,0:T(8,128)(2,1)S(1)}, bf16[128,1024]{1,0:T(8,128)(2,1)}, u32[]{:S(2)}) %copy-start.2) | copy-done | bytes 262168
  2.5 0.0 copy-start.3
  2.5 0.8 %copy-done.3 = bf16[4,32,256]{2,1,0:T(8,128)(2,1)S(1)} copy-done((bf16[4,32,256]{2,1,0:T(8,128)(2,1)S(1)}, bf16[4,32,256]{2,1,0:T(8,128)(2,1)}, u32[]{:S(2)}) %copy-start.3) | copy-done | bytes 65560
  3.4 40.2 %gather_images.1 = (bf16[12,128,256]{2,1,0:T(8,128)(2,1)S(1)}, bf16[8,256,256]{2,1,0:T(8,128)(2,1)S(1)}, f32[1024,128]{1,0:T(8,128)S(1)}, s32[1,128]{1,0:T(1,128...) custom-call(s32[64]{0:T(128)S(1)} %copy-done.4, bf16[128,256]{1,0:T(8,128)(2,1)S(1)} %bitcast.14, ...), custom_call_target="tpu_custom_call" | custom-call | tf_op jit(solution)/shard_map/gather_images/pallas_call | solution.py:491
  43.6 0.0 copy-start.6
  43.6 0.6 copy-done.6
  44.3 7.2 %pair_gradients.1 = (bf16[1536,256]{1,0:T(8,128)(2,1)S(1)}, bf16[2048,256]{1,0:T(8,128)(2,1)S(1)}) custom-call(s32[1,128]{1,0:T(1,128)S(1)} %bitcast.16, s32[1,128]{1,0:T(1,128)S(1)} %get-tuple-element.13.place_ref, bf16[1536,256]{1,0:T(8,128)(2,1)S(1)} %bitcast.12, bf16[2048,256]{1,0:T(8,128)(2,1)S(1)} %bitcast.10, f32[1024,128]{1,0:T(8,128)S(1)} %get-tuple-element.16.laid), custom_call_target="tpu_custom_call" | custom-call | tf_op jit(solution)/shard_map/pair_gradients/pallas_call | solution.py:520
  51.4 0.0 copy-start.1
  51.4 29.8 %return_gradients.1 = bf16[128,256]{1,0:T(8,128)(2,1)S(1)} custom-call(bf16[8,256,256]{2,1,0:T(8,128)(2,1)S(1)} %bitcast.11, bf16[12,128,256]{2,1,0:T(8,128)(2,1)S(1)} %bitcast.13, f32[8,8,256]{2,1,0:T(8,128)S(1)} %get-tuple-element.19.pick_rows, f32[128,256]{1,0:T(8,128)S(1)} %get-tuple-element.20.feature), custom_call_target="tpu_custom_call" | custom-call | tf_op jit(solution)/shard_map/return_gradients/pallas_call | solution.py:542
  81.3 0.0 copy-done.1
  81.3 0.8 %convolution_convert_fusion = bf16[128,256]{1,0:T(8,128)(2,1)} fusion(bf16[128,256]{1,0:T(8,128)(2,1)S(1)} %return_gradients.1, bf16[256,256]{1,0:T(8,128)(2,1)S(1)} %copy-done.1), kind=kOutput, calls=%fused_computation | convolution fusion | flops 16809984 | bytes 262144 | tf_op jit(solution)/shard_map/dot_general | solution.py:566
Async XLA Ops:
  0.0 0.7 copy-start.4
  0.0 0.7 copy-start.5
  0.7 0.9 %copy-start = (bf16[256,256]{1,0:T(8,128)(2,1)S(1)}, bf16[256,256]{1,0:T(8,128)(2,1)}, u32[]{:S(2)}) copy-start(bf16[256,256]{1,0:T(8,128)(2,1)} %weight.1) | copy-start | bytes 393220
  1.6 0.9 %copy-start.2 = (bf16[128,1024]{1,0:T(8,128)(2,1)S(1)}, bf16[128,1024]{1,0:T(8,128)(2,1)}, u32[]{:S(2)}) copy-start(bf16[128,1024]{1,0:T(8,128)(2,1)} %grads.1) | copy-start | bytes 786436
  2.5 0.8 %copy-start.3 = (bf16[4,32,256]{2,1,0:T(8,128)(2,1)S(1)}, bf16[4,32,256]{2,1,0:T(8,128)(2,1)}, u32[]{:S(2)}) copy-start(bf16[4,32,256]{2,1,0:T(8,128)(2,1)} %param.6) | copy-start | bytes 196612
  43.6 0.7 copy-start.6
  51.4 29.9 %copy-start.1 = (bf16[256,256]{1,0:T(8,128)(2,1)S(1)}, bf16[256,256]{1,0:T(8,128)(2,1)}, u32[]{:S(2)}) copy-start(bf16[256,256]{1,0:T(8,128)(2,1)} %weight.1) | copy-start | bytes 393220

commit v2 on v1

--- a/solution.py
+++ b/solution.py
@@ -13,6 +13,8 @@
 LANES = 128
 VMEM_LIMIT = 40 * 1024 * 1024
 GRID = (4, 8, 2)
+STEPS_Y = {1: 0, 2: 0, 3: 2, 4: 2}
+STEPS_Z = {2: 0, 1: 0, 4: 2, 3: 2, 6: 4, 5: 4}
 
 
 def place_of(offset, ring):
@@ -47,9 +49,13 @@
     def across(self, turn):
         return {"grp": self.group(self.s_at(turn), self.y)}
 
-    def greet(self):
+    def greet(self, steps_y, steps_z):
         barrier = pltpu.get_barrier_semaphore()
-        others = [self.along_y(1), self.along_y(-1), self.along_z(1), self.along_z(-1)]
+        others = []
+        for hop in sorted({distance - before for distance, before in steps_y.items()}):
+            others += [self.along_y(hop), self.along_y(-hop)]
+        for hop in sorted({distance - before for distance, before in steps_z.items()}):
+            others += [self.along_z(hop), self.along_z(-hop)]
         others += [self.across(turn) for turn in range(1, self.peers)]
         for other in others:
             pl.semaphore_signal(barrier, inc=1, device_id=other, device_id_type=MESH)
@@ -90,21 +96,33 @@
 def gather_kernel(
     grid,
     ring_z,
+    steps_y,
+    steps_z,
     images,
     length,
+    picks_arg,
+    tokens_arg,
+    weight_arg,
+    grads_arg,
+    firsts_arg,
+    seconds_arg,
+    pool,
+    received,
+    laid,
+    firsts,
+    places,
+    pick_rows,
+    feature,
+    pool_zero,
+    slot_zero,
     picks,
     tokens,
     weight,
     grads,
     seconds,
-    pool,
-    received,
-    laid,
-    places,
-    pick_rows,
-    feature,
     blocks,
     stage,
+    fetch_sem,
     y_send,
     y_recv,
     z_send,
@@ -116,8 +134,25 @@
     ring_y, peers = here.ring_y, here.peers
     rows, width = tokens.shape
     block_rows = blocks.shape[1]
-    met = here.greet()
-
+    fetches = [
+        pltpu.make_async_copy(src, dst, fetch_sem.at[n])
+        for n, (src, dst) in enumerate(
+            (
+                (tokens_arg, tokens),
+                (weight_arg, weight),
+                (picks_arg, picks),
+                (seconds_arg, seconds),
+                (firsts_arg, firsts),
+                (grads_arg, grads),
+            )
+        )
+    ]
+    for fetch in fetches:
+        fetch.start()
+    met = here.greet(steps_y, steps_z)
+
+    for fetch in fetches[:3]:
+        fetch.wait()
     projected = jnp.dot(tokens[...], weight[...], preferred_element_type=jnp.float32)
     feature[...] = projected
     mean_square = jnp.mean(projected * projected, axis=-1, keepdims=True)
@@ -136,37 +171,38 @@
     met()
 
     half_y, half_z = ring_y // 2, ring_z // 2
-    y_copies, z_copies, x_copies = [], [], []
-
-    def forward_y(step):
-        for way, turn in enumerate((1, -1)):
-            part = slice(0, block_rows)
-            if step == half_y:
-                part = slice(0, rows // 2) if way == 0 else slice(rows // 2, block_rows)
-            part = pl.ds(part.start, part.stop - part.start)
-            y_copies.append(
-                send(
-                    blocks.at[place_of(-turn * (step - 1), ring_y), part],
-                    blocks.at[place_of(-turn * step, ring_y), part],
-                    y_send.at[way, step - 1],
-                    y_recv.at[way, step - 1],
-                    here.along_y(turn),
+    y_copies, z_copies, x_copies = {}, {}, []
+
+    def forward_y(source):
+        for distance, before in steps_y.items():
+            if before != source:
+                continue
+            for way, turn in enumerate((1, -1)):
+                part = pl.ds(0, block_rows)
+                if distance == half_y:
+                    part = pl.ds(0, rows // 2) if way == 0 else pl.ds(rows // 2, block_rows - rows // 2)
+                y_copies[distance, way] = send(
+                    blocks.at[place_of(-turn * before, ring_y), part],
+                    blocks.at[place_of(-turn * distance, ring_y), part],
+                    y_send.at[way, distance - 1],
+                    y_recv.at[way, distance - 1],
+                    here.along_y(turn * (distance - before)),
                 )
-            )
-
-    def forward_z(step):
-        for way, turn in enumerate((1, -1)):
-            part = pl.ds(0, rows) if step < half_z else pl.ds(way * (rows // 2), rows // 2)
-            owner = here.z_at(-turn * (step - 1))
-            z_copies.append(
-                send(
+
+    def forward_z(source):
+        for distance, before in steps_z.items():
+            if before != source:
+                continue
+            for way, turn in enumerate((1, -1)):
+                part = pl.ds(way * (rows // 2), rows // 2) if distance == half_z else pl.ds(0, rows)
+                owner = here.z_at(-turn * before)
+                z_copies[distance, way] = send(
                     pool.at[owner, part],
                     pool.at[owner, part],
-                    z_send.at[way, step - 1],
-                    z_recv.at[way, step - 1],
-                    here.along_z(turn),
+                    z_send.at[way, distance - 1],
+                    z_recv.at[way, distance - 1],
+                    here.along_z(turn * (distance - before)),
                 )
-            )
 
     own = rows_at(here.s, length)
 
@@ -194,10 +230,12 @@
         for at in range(place, place + count):
             received[at, own] = stage[at, own]
 
-    forward_y(1)
-    forward_z(1)
+    forward_y(0)
+    forward_z(0)
     plan = batches(ring_y)
     choose(0, *plan[0])
+    for fetch in fetches[3:]:
+        fetch.wait()
 
     slot = seconds[...]
     offset = lax.rem(lax.rem(lax.div(slot, here.cores), ring_y) - here.y + ring_y, ring_y)
@@ -224,26 +262,26 @@
 
     tiles = grads.shape[1] // LANES
     todo = list(range(tiles))
-    for step in range(1, max(half_y, half_z) + 1):
+    for distance in range(1, max(half_y, half_z) + 1):
         if todo:
             lay(todo.pop(0))
-        if step <= half_y:
-            for copy in y_copies[2 * step - 2 : 2 * step]:
-                copy.wait_recv()
-            if step < half_y:
-                forward_y(step + 1)
-        if step <= half_z:
-            for copy in z_copies[2 * step - 2 : 2 * step]:
-                copy.wait_recv()
-            if step < half_z:
-                forward_z(step + 1)
-        if step <= half_y:
-            choose(step, *plan[step])
+        if distance <= half_y:
+            for way in range(2):
+                y_copies[distance, way].wait_recv()
+            forward_y(distance)
+        if distance <= half_z:
+            for way in range(2):
+                z_copies[distance, way].wait_recv()
+            forward_z(distance)
+        if distance <= half_y:
+            choose(distance, *plan[distance])
     for tile in todo:
         lay(tile)
+    pool_zero[...] = jnp.zeros_like(pool_zero)
+    slot_zero[...] = jnp.zeros_like(slot_zero)
     for copy in x_copies:
         copy.wait_recv()
-    for copy in y_copies + z_copies + x_copies:
+    for copy in [*y_copies.values(), *z_copies.values(), *x_copies]:
         copy.wait_send()
 
 
@@ -254,8 +292,8 @@
     pool,
     received,
     laid,
-    pool_part,
-    slot_part,
+    pool_zero,
+    slot_zero,
     pool_total,
     slot_total,
 ):
@@ -266,8 +304,7 @@
     scale = 1.0 / (width * SOFTMAX_COOLING)
     together = 4
 
-    pool_total[...] = jnp.zeros_like(pool_total)
-    slot_total[...] = jnp.zeros_like(slot_total)
+    del pool_zero, slot_zero
     side = (LANES, LANES)
     row_block = lax.div(lax.broadcasted_iota(jnp.int32, side, 0), length)
     lane_block = lax.div(lax.broadcasted_iota(jnp.int32, side, 1), length)
@@ -328,20 +365,22 @@
         return carry
 
     lax.fori_loop(0, groups // together, step, 0)
-    pool_part[...] = pool_total[...].astype(jnp.bfloat16)
-    slot_part[...] = slot_total[...].astype(jnp.bfloat16)
 
 
 def return_kernel(
     grid,
     ring_z,
+    steps_y,
+    steps_z,
     images,
     length,
-    slots,
-    pool,
+    slot_total,
+    pool_total,
     pick_rows,
     feature,
     feature_grad,
+    slots,
+    pool,
     arrived,
     choosers,
     y_in,
@@ -359,40 +398,49 @@
     ring_y, peers = here.ring_y, here.peers
     rows, width = feature.shape
     half_y, half_z = ring_y // 2, ring_z // 2
-    met = here.greet()
+    met = here.greet(steps_y, steps_z)
     own = rows_at(here.s, length)
     plan = batches(ring_y)
+    slots[...] = slot_total[...].astype(jnp.bfloat16)
+    pool[...] = pool_total[...].astype(jnp.bfloat16)
     met()
 
-    y_copies, z_copies, x_copies = [], [], {}
-
-    def ring_z_send(step, source_of):
+    y_copies, z_copies, x_copies = {}, {}, {}
+
+    def part_of(distance, way, half):
+        return pl.ds(way * (rows // 2), rows // 2) if distance == half else pl.ds(0, rows)
+
+    def send_z(distance):
+        hop = distance - steps_z[distance]
         for way, turn in enumerate((1, -1)):
-            part = pl.ds(way * (rows // 2), rows // 2) if step == 1 else pl.ds(0, rows)
-            z_copies.append(
-                send(
-                    source_of(way, turn).at[part],
-                    z_in.at[way, step - 1, part],
-                    z_send.at[way, step - 1],
-                    z_recv.at[way, step - 1],
-                    here.along_z(turn),
-                )
-            )
-
-    def ring_y_send(step):
+            part = part_of(distance, way, half_z)
+            if distance in steps_z.values():
+                source = z_out.at[way, distance - 1, part]
+            else:
+                source = pool.at[here.z_at(turn * distance), part]
+            z_copies[distance, way] = send(
+                source,
+                z_in.at[way, distance - 1, part],
+                z_send.at[way, distance - 1],
+                z_recv.at[way, distance - 1],
+                here.along_z(turn * hop),
+            )
+
+    def send_y(distance):
+        hop = distance - steps_y[distance]
         for way, turn in enumerate((1, -1)):
-            part = pl.ds(way * (rows // 2), rows // 2) if step == 1 else pl.ds(0, rows)
-            y_copies.append(
-                send(
-                    y_out.at[way, step - 1, part],
-                    y_in.at[way, step - 1, part],
-                    y_send.at[way, step - 1],
-                    y_recv.at[way, step - 1],
-                    here.along_y(turn),
-                )
-            )
-
-    ring_z_send(1, lambda way, turn: pool.at[here.z_at(turn * half_z)])
+            part = part_of(distance, way, half_y)
+            y_copies[distance, way] = send(
+                y_out.at[way, distance - 1, part],
+                y_in.at[way, distance - 1, part],
+                y_send.at[way, distance - 1],
+                y_recv.at[way, distance - 1],
+                here.along_y(turn * hop),
+            )
+
+    for distance in range(half_z, 0, -1):
+        if distance not in steps_z.values():
+            send_z(distance)
     for distance in range(half_y, -1, -1):
         place, count = plan[distance]
         x_copies[distance] = [
@@ -416,52 +464,51 @@
         for copy in x_copies[distance]:
             copy.wait_recv()
 
-    def joined(total, ins, way, step):
-        if step > 1:
-            return total + ins[way, step - 1].astype(jnp.float32)
+    def joined(total, ins, way, distance, half):
+        if distance < half:
+            return total + ins[way, distance - 1].astype(jnp.float32)
         low = way * (rows // 2)
-        added = total[low : low + rows // 2] + ins[way, 0, low : low + rows // 2].astype(jnp.float32)
+        added = ins[way, distance - 1, low : low + rows // 2].astype(jnp.float32)
+        added = added + total[low : low + rows // 2]
         rest = total[rows // 2 :] if way == 0 else total[: rows // 2]
         return jnp.concatenate([added, rest] if way == 0 else [rest, added], axis=0)
 
-    for step in range(1, max(half_y, half_z) + 1):
-        if 1 < step <= half_z:
-            for copy in z_copies[2 * step - 4 : 2 * step - 2]:
-                copy.wait_recv()
+    def collect(total, way, distance, steps, copies, ins, half):
+        for farther in sorted(steps, reverse=True):
+            if steps[farther] == distance:
+                copies[farther, way].wait_recv()
+                total = joined(total, ins, way, farther, half)
+        return total
+
+    along_z = (steps_z, z_copies, z_in, half_z)
+    along_y = (steps_y, y_copies, y_in, half_y)
+    for distance in range(max(half_y, half_z), 0, -1):
+        if distance <= half_y:
+            wait_x(distance)
             for way, turn in enumerate((1, -1)):
-                mine = pool[here.z_at(turn * (half_z - step + 1))].astype(jnp.float32)
-                z_out[way, step - 1] = joined(mine, z_in, way, step - 1).astype(jnp.bfloat16)
-            ring_z_send(step, lambda way, turn: z_out.at[way, step - 1])
-        if step <= half_y:
-            distance = half_y - step + 1
-            wait_x(distance)
-            if step == 1:
-                total = summed(ring_y - 1)
-                for way in range(2):
-                    y_out[way, 0] = total.astype(jnp.bfloat16)
-            else:
-                totals = [summed(place_of(turn * distance, ring_y)) for turn in (1, -1)]
-                for copy in y_copies[2 * step - 4 : 2 * step - 2]:
-                    copy.wait_recv()
-                for way in range(2):
-                    y_out[way, step - 1] = joined(totals[way], y_in, way, step - 1).astype(
-                        jnp.bfloat16
-                    )
-            ring_y_send(step)
+                if distance < half_y or way == 0:
+                    mine = summed(place_of(turn * distance, ring_y))
+                total = collect(mine, way, distance, *along_y)
+                y_out[way, distance - 1] = total.astype(jnp.bfloat16)
+            send_y(distance)
+        if distance <= half_z and distance in steps_z.values():
+            for way, turn in enumerate((1, -1)):
+                mine = pool[here.z_at(turn * distance)].astype(jnp.float32)
+                total = collect(mine, way, distance, *along_z)
+                z_out[way, distance - 1] = total.astype(jnp.bfloat16)
+            send_z(distance)
     wait_x(0)
     gradient = summed(0) + pool[here.z].astype(jnp.float32)
     projected = feature[...]
     mean_square = jnp.mean(projected * projected, axis=-1, keepdims=True)
     inv_rms = lax.rsqrt(mean_square + EPSILON)
     normed = projected * inv_rms
-    for copy in y_copies[2 * half_y - 2 :] + z_copies[2 * half_z - 2 :]:
-        copy.wait_recv()
     for way in range(2):
-        gradient = joined(gradient, y_in, way, half_y)
-        gradient = joined(gradient, z_in, way, half_z)
+        gradient = collect(gradient, way, 0, *along_z)
+        gradient = collect(gradient, way, 0, *along_y)
     mean = jnp.mean(gradient * normed, axis=-1, keepdims=True)
     feature_grad[...] = (inv_rms * (gradient - normed * mean)).astype(jnp.bfloat16)
-    for copy in y_copies + z_copies + sum(x_copies.values(), []):
+    for copy in [*y_copies.values(), *z_copies.values(), *sum(x_copies.values(), [])]:
         copy.wait_send()
 
 
@@ -479,30 +526,52 @@
     return [dma(shape) for shape in pairs for _ in range(2)]
 
 
-def local(grid, ring_z, tokens, proj_weight, match_grad, edge_first, pair_second_image, send_pick):
+def local(
+    grid,
+    ring_z,
+    steps_y,
+    steps_z,
+    tokens,
+    proj_weight,
+    match_grad,
+    edge_first,
+    pair_second_image,
+    send_pick,
+):
     images, length, width = tokens.shape
     rows = images * length
     pairs = edge_first.shape[0]
     ring_y, peers = grid[1], grid[0] * grid[2]
     half_y, half_z = ring_y // 2, ring_z // 2
+    layout = (grid, ring_z, steps_y, steps_z, images, length)
     bf16, f32 = jnp.bfloat16, jnp.float32
     shape = jax.ShapeDtypeStruct
-
-    pool, received, laid, places, pick_rows, feature = pl.pallas_call(
-        functools.partial(gather_kernel, grid, ring_z, images, length),
+    pool_rows, slot_rows = ring_z * rows, ring_y * peers * length
+
+    pool, received, laid, firsts, places, pick_rows, feature, pool_zero, slot_zero = pl.pallas_call(
+        functools.partial(gather_kernel, *layout),
         out_shape=(
             shape((ring_z, rows, width), bf16),
             shape((ring_y, peers * length, width), bf16),
             shape((pairs * length * length // LANES, LANES), f32),
             shape((1, pairs), jnp.int32),
+            shape((1, pairs), jnp.int32),
             shape((ring_y, 8, peers * length), f32),
             shape((rows, width), f32),
+            shape((pool_rows, width), f32),
+            shape((slot_rows, width), f32),
         ),
-        in_specs=in_smem(1) + in_vmem(4),
-        out_specs=tuple(in_vmem(6)),
+        in_specs=[pl.BlockSpec(memory_space=pltpu.HBM)] * 6,
+        out_specs=tuple(in_vmem(9)),
         scratch_shapes=[
+            pltpu.SMEM((send_pick.shape[0],), jnp.int32),
+            pltpu.VMEM((rows, width), bf16),
+            pltpu.VMEM(proj_weight.shape, bf16),
+            pltpu.VMEM(match_grad.shape, bf16),
+            pltpu.VMEM((1, pairs), jnp.int32),
             pltpu.VMEM((ring_y, rows + 16, width), bf16),
             pltpu.VMEM((ring_y, peers * length, width), bf16),
+            pltpu.SemaphoreType.DMA((6,)),
             *ring_semaphores(half_y, half_z, peers),
         ],
         compiler_params=pltpu.CompilerParams(
@@ -510,41 +579,45 @@
         ),
         name="gather_images",
     )(
-        send_pick,
-        tokens.reshape(rows, width),
-        proj_weight,
-        match_grad,
-        pair_second_image.reshape(1, pairs),
+        *(
+            pltpu.with_memory_space_constraint(argument, pltpu.HBM)
+            for argument in (
+                send_pick,
+                tokens.reshape(rows, width),
+                proj_weight,
+                match_grad,
+                edge_first.reshape(1, pairs),
+                pair_second_image.reshape(1, pairs),
+            )
+        )
     )
 
-    pool_part, slot_part = pl.pallas_call(
+    pool_total, slot_total = pl.pallas_call(
         functools.partial(pair_kernel, length),
-        out_shape=(
-            shape((ring_z * rows, width), bf16),
-            shape((ring_y * peers * length, width), bf16),
-        ),
-        in_specs=in_smem(2) + in_vmem(3),
+        out_shape=(shape((pool_rows, width), f32), shape((slot_rows, width), f32)),
+        in_specs=in_smem(2) + in_vmem(5),
         out_specs=tuple(in_vmem(2)),
-        scratch_shapes=[
-            pltpu.VMEM((ring_z * rows, width), f32),
-            pltpu.VMEM((ring_y * peers * length, width), f32),
-        ],
+        input_output_aliases={5: 0, 6: 1},
         compiler_params=pltpu.CompilerParams(vmem_limit_bytes=VMEM_LIMIT),
         name="pair_gradients",
     )(
-        edge_first.reshape(1, pairs),
+        firsts,
         places,
-        pool.reshape(ring_z * rows, width),
-        received.reshape(ring_y * peers * length, width),
+        pool.reshape(pool_rows, width),
+        received.reshape(slot_rows, width),
         laid,
+        pool_zero,
+        slot_zero,
     )
 
     feature_grad = pl.pallas_call(
-        functools.partial(return_kernel, grid, ring_z, images, length),
+        functools.partial(return_kernel, *layout),
         out_shape=shape((rows, width), bf16),
         in_specs=in_vmem(4),
         out_specs=pl.BlockSpec(memory_space=pltpu.VMEM),
         scratch_shapes=[
+            pltpu.VMEM((ring_y, peers * length, width), bf16),
+            pltpu.VMEM((ring_z, rows, width), bf16),
             pltpu.VMEM((ring_y, peers * length, width), bf16),
             pltpu.VMEM((ring_y, rows, peers * length), bf16),
             pltpu.VMEM((2, half_y, rows, width), bf16),
@@ -558,8 +631,8 @@
         ),
         name="return_gradients",
     )(
-        slot_part.reshape(ring_y, peers * length, width),
-        pool_part.reshape(ring_z, rows, width),
+        slot_total.reshape(ring_y, peers * length, width),
+        pool_total.reshape(ring_z, rows, width),
         pick_rows,
         feature,
     )
@@ -569,7 +642,7 @@
     return token_grad.astype(bf16).reshape(images, length, width)
 
 
-def solution(mesh, grid=GRID):
+def solution(mesh, grid=GRID, steps_y=STEPS_Y, steps_z=STEPS_Z):
     placed = (
         P(("grp", "sub"), None, None),
         P(),
@@ -579,7 +652,7 @@
         P(("grp", "sub")),
     )
     return jax.shard_map(
-        functools.partial(local, grid, mesh.shape["sub"]),
+        functools.partial(local, grid, mesh.shape["sub"], steps_y, steps_z),
         mesh=mesh,
         in_specs=placed,
         out_specs=P(("grp", "sub"), None, None),

time: 82.4 us -> 69.7 us (0.85)
  the two profiles are of different devices: /device:TPU:16 before, /device:TPU:1 now
where the time goes in v2:
time: 69.7 us; the launch traced here: 69.6 us
  Pallas kernels  68.7 us (99%)
  matrix products  0.83 us (1%)
    pallas_call x1, Pallas kernels, local(): pl.pallas_call(functools.partial(gather_kernel, *layout), out_shape=(shap...  39 us
    pallas_call x1, Pallas kernels, local(): pl.pallas_call(functools.partial(return_kernel, *layout), out_shape=shape...  22.9 us
    pallas_call x1, Pallas kernels, local(): pl.pallas_call(functools.partial(pair_kernel, length), out_shape=(shape((...  6.78 us

profile of v2, /device:TPU:1, one launch (start us, length us, event | category | flops | bytes accessed | tf_op | source)
XLA Modules:
  0.0 69.6 jit_solution(15653813740936422042)
XLA Ops:
  0.0 39.0 %gather_images.1 = (bf16[12,128,256]{2,1,0:T(8,128)(2,1)S(1)}, bf16[8,256,256]{2,1,0:T(8,128)(2,1)S(1)}, f32[1024,128]{1,0:T(8,128)S(1)}, s32[1,128]{1,0:T(1,128...) custom-call(s32[64]{0:T(128)} %picks_arg.1, ...), custom_call_target="tpu_custom_call" | custom-call | tf_op jit(solution)/shard_map/gather_images/pallas_call | solution.py:551
  39.0 6.8 %pair_gradients.1 = (f32[1536,256]{1,0:T(8,128)S(1)}, f32[2048,256]{1,0:T(8,128)S(1)}) custom-call(s32[1,128]{1,0:T(1,128)S(1)} %get-tuple-element.16.first_ref, s32[1,128]{1,0:T(1,128)S(1)} %get-tuple-element.17.place_ref, bf16[1536,256]{1,0:T(8,128)(2,1)S(1)} %bitcast.13, ...), custom_call_target="tpu_custom_call", output_to_operand_aliasing={{0}: (5, {}), {1}: (6, {})} | custom-call | tf_op jit(solution)/shard_map/pair_gradients/pallas_call | solution.py:595
  45.8 0.0 copy-start
  45.8 22.9 %return_gradients.1 = bf16[128,256]{1,0:T(8,128)(2,1)S(1)} custom-call(f32[8,256,256]{2,1,0:T(8,128)S(1)} %bitcast.10, f32[12,128,256]{2,1,0:T(8,128)S(1)} %bitcast.11, f32[8,8,256]{2,1,0:T(8,128)S(1)} %get-tuple-element.25.pick_rows, f32[128,256]{1,0:T(8,128)S(1)} %get-tuple-element.26.feature), custom_call_target="tpu_custom_call" | custom-call | tf_op jit(solution)/shard_map/return_gradients/pallas_call | solution.py:613
  68.7 0.0 copy-done
  68.7 0.8 %convolution_convert_fusion = bf16[128,256]{1,0:T(8,128)(2,1)} fusion(bf16[128,256]{1,0:T(8,128)(2,1)S(1)} %return_gradients.1, bf16[256,256]{1,0:T(8,128)(2,1)S(1)} %copy-done), kind=kOutput, calls=%fused_computation | convolution fusion | flops 16809984 | bytes 262144 | tf_op jit(solution)/shard_map/dot_general | solution.py:639
Async XLA Ops:
  45.8 22.9 %copy-start = (bf16[256,256]{1,0:T(8,128)(2,1)S(1)}, bf16[256,256]{1,0:T(8,128)(2,1)}, u32[]{:S(2)}) copy-start(bf16[256,256]{1,0:T(8,128)(2,1)} %weight_arg.1) | copy-start | bytes 393220

commit v3 on v2

--- a/solution.py
+++ b/solution.py
@@ -78,6 +78,10 @@
 def batches(ring):
     half = ring // 2
     return [(0, 1)] + [(2 * d - 1, 2) for d in range(1, half)] + [(ring - 1, 1)]
+
+
+def spread(count):
+    return (count // 8 | 1) * 8
 
 
 def rows_at(index, count):
@@ -113,8 +117,6 @@
     places,
     pick_rows,
     feature,
-    pool_zero,
-    slot_zero,
     picks,
     tokens,
     weight,
@@ -258,7 +260,7 @@
                 moved = pltpu.roll(parts[q], shift, 1) if shift else parts[q]
                 total = moved if total is None else jnp.where(lane_block == q, moved, total)
             i = tile * across + r
-            laid[i * groups : (i + 1) * groups] = total
+            laid[i * spread(groups) : i * spread(groups) + groups] = total
 
     tiles = grads.shape[1] // LANES
     todo = list(range(tiles))
@@ -277,34 +279,20 @@
             choose(distance, *plan[distance])
     for tile in todo:
         lay(tile)
-    pool_zero[...] = jnp.zeros_like(pool_zero)
-    slot_zero[...] = jnp.zeros_like(slot_zero)
     for copy in x_copies:
         copy.wait_recv()
     for copy in [*y_copies.values(), *z_copies.values(), *x_copies]:
         copy.wait_send()
 
 
-def pair_kernel(
-    length,
-    first_ref,
-    place_ref,
-    pool,
-    received,
-    laid,
-    pool_zero,
-    slot_zero,
-    pool_total,
-    slot_total,
-):
+def pair_gradients(length, first_ref, place_ref, pool, received, laid, by_first, by_second):
     pairs = first_ref.shape[1]
     across = LANES // length
     groups = pairs // across
-    width = pool.shape[1]
+    width = pool.shape[2]
     scale = 1.0 / (width * SOFTMAX_COOLING)
-    together = 4
-
-    del pool_zero, slot_zero
+    together = min(8, groups)
+
     side = (LANES, LANES)
     row_block = lax.div(lax.broadcasted_iota(jnp.int32, side, 0), length)
     lane_block = lax.div(lax.broadcasted_iota(jnp.int32, side, 1), length)
@@ -321,13 +309,12 @@
         )
 
     def step(chunk, carry):
-        firsts, seconds, f_at, s_at, scores, incoming = [], [], [], [], [], []
+        firsts, seconds, scores, incoming = [], [], [], []
         for n in range(together):
             g = chunk * together + n
-            f_at.append([rows_at(first_ref[0, q * groups + g], length) for q in range(across)])
-            s_at.append([rows_at(place_ref[0, q * groups + g], length) for q in range(across)])
-            firsts.append(jnp.concatenate([pool[at] for at in f_at[n]], axis=0))
-            seconds.append(jnp.concatenate([received[at] for at in s_at[n]], axis=0))
+            pairs_of_g = [q * groups + g for q in range(across)]
+            firsts.append(jnp.concatenate([pool[first_ref[0, e]] for e in pairs_of_g], axis=0))
+            seconds.append(jnp.concatenate([received[place_ref[0, e]] for e in pairs_of_g], axis=0))
             full = lax.dot_general(
                 firsts[n],
                 seconds[n],
@@ -338,7 +325,7 @@
             for q in range(1, across):
                 packed = jnp.where(narrow == q, full[q * length : (q + 1) * length], packed)
             scores.append(packed)
-            incoming.append(laid[pl.ds(g, length, stride=groups), :])
+            incoming.append(laid[pl.ds(g, length, stride=spread(groups)), :])
         shape = (together, length, LANES)
         expo = jnp.exp(jnp.concatenate(scores, axis=0) * scale)
         gradient = jnp.concatenate(incoming, axis=0)
@@ -360,11 +347,45 @@
             )
             for q in range(across):
                 part = slice(q * length, (q + 1) * length)
-                pool_total[f_at[n][q]] += grad_first[part]
-                slot_total[s_at[n][q]] += grad_second[part]
+                rows_of_pair = pl.ds(q * groups + chunk * together + n, length, stride=spread(pairs))
+                for h in range(width // LANES):
+                    lanes = slice(h * LANES, (h + 1) * LANES)
+                    by_first[h, rows_of_pair, :] = grad_first[part, lanes]
+                    by_second[h, rows_of_pair, :] = grad_second[part, lanes]
         return carry
 
     lax.fori_loop(0, groups // together, step, 0)
+
+
+def add_up(length, image_of_pair, by_pair, total, rounded):
+    pairs = image_of_pair.shape[1]
+    far = spread(length)
+    halves, count = total.shape[0], total.shape[1] // far
+    image = lax.broadcasted_iota(jnp.int32, (count, pairs), 0)
+    chosen = jnp.where(image == image_of_pair[...], 1.0, 0.0).astype(jnp.bfloat16)
+    together = length
+
+    def step(chunk, carry):
+        for n in range(together):
+            i = chunk * together + n
+            rows_of_i = pl.ds(pl.multiple_of(i * spread(pairs), 8), pairs)
+            rows_of_i = [by_pair[h, rows_of_i].astype(jnp.bfloat16) for h in range(halves)]
+            sums = jnp.dot(
+                chosen, jnp.concatenate(rows_of_i, axis=1), preferred_element_type=jnp.float32
+            )
+            for h in range(halves):
+                lanes = slice(h * LANES, (h + 1) * LANES)
+                total[h, pl.ds(i, count, stride=far), :] = sums[:, lanes]
+        return carry
+
+    lax.fori_loop(0, length // together, step, 0)
+    images = rounded.shape[1] // length
+    for n in range(count):
+        rows_of_image = slice(n % images * length, (n % images + 1) * length)
+        for h in range(halves):
+            rounded[n // images, rows_of_image, h * LANES : (h + 1) * LANES] = total[
+                h, n * far : n * far + length
+            ].astype(jnp.bfloat16)
 
 
 def return_kernel(
@@ -374,11 +395,20 @@
     steps_z,
     images,
     length,
-    slot_total,
-    pool_total,
+    first_ref,
+    place_ref,
+    firsts,
+    places,
+    pool_images,
+    received,
+    laid,
     pick_rows,
     feature,
     feature_grad,
+    by_first,
+    by_second,
+    pool_total,
+    slot_total,
     slots,
     pool,
     arrived,
@@ -401,8 +431,10 @@
     met = here.greet(steps_y, steps_z)
     own = rows_at(here.s, length)
     plan = batches(ring_y)
-    slots[...] = slot_total[...].astype(jnp.bfloat16)
-    pool[...] = pool_total[...].astype(jnp.bfloat16)
+    pair_gradients(
+        length, first_ref, place_ref, pool_images, received, laid, by_first, by_second
+    )
+    add_up(length, firsts, by_first, pool_total, pool)
     met()
 
     y_copies, z_copies, x_copies = {}, {}, {}
@@ -441,6 +473,7 @@
     for distance in range(half_z, 0, -1):
         if distance not in steps_z.values():
             send_z(distance)
+    add_up(length, places, by_second, slot_total, slots)
     for distance in range(half_y, -1, -1):
         place, count = plan[distance]
         x_copies[distance] = [
@@ -548,21 +581,19 @@
     shape = jax.ShapeDtypeStruct
     pool_rows, slot_rows = ring_z * rows, ring_y * peers * length
 
-    pool, received, laid, firsts, places, pick_rows, feature, pool_zero, slot_zero = pl.pallas_call(
+    pool, received, laid, firsts, places, pick_rows, feature = pl.pallas_call(
         functools.partial(gather_kernel, *layout),
         out_shape=(
             shape((ring_z, rows, width), bf16),
             shape((ring_y, peers * length, width), bf16),
-            shape((pairs * length * length // LANES, LANES), f32),
+            shape((length * spread(pairs * length // LANES), LANES), f32),
             shape((1, pairs), jnp.int32),
             shape((1, pairs), jnp.int32),
             shape((ring_y, 8, peers * length), f32),
             shape((rows, width), f32),
-            shape((pool_rows, width), f32),
-            shape((slot_rows, width), f32),
         ),
         in_specs=[pl.BlockSpec(memory_space=pltpu.HBM)] * 6,
-        out_specs=tuple(in_vmem(9)),
+        out_specs=tuple(in_vmem(7)),
         scratch_shapes=[
             pltpu.SMEM((send_pick.shape[0],), jnp.int32),
             pltpu.VMEM((rows, width), bf16),
@@ -592,30 +623,16 @@
         )
     )
 
-    pool_total, slot_total = pl.pallas_call(
-        functools.partial(pair_kernel, length),
-        out_shape=(shape((pool_rows, width), f32), shape((slot_rows, width), f32)),
-        in_specs=in_smem(2) + in_vmem(5),
-        out_specs=tuple(in_vmem(2)),
-        input_output_aliases={5: 0, 6: 1},
-        compiler_params=pltpu.CompilerParams(vmem_limit_bytes=VMEM_LIMIT),
-        name="pair_gradients",
-    )(
-        firsts,
-        places,
-        pool.reshape(pool_rows, width),
-        received.reshape(slot_rows, width),
-        laid,
-        pool_zero,
-        slot_zero,
-    )
-
     feature_grad = pl.pallas_call(
         functools.partial(return_kernel, *layout),
         out_shape=shape((rows, width), bf16),
-        in_specs=in_vmem(4),
+        in_specs=in_smem(2) + in_vmem(7),
         out_specs=pl.BlockSpec(memory_space=pltpu.VMEM),
         scratch_shapes=[
+            pltpu.VMEM((width // LANES, length * spread(pairs), LANES), f32),
+            pltpu.VMEM((width // LANES, length * spread(pairs), LANES), f32),
+            pltpu.VMEM((width // LANES, pool_rows // length * spread(length), LANES), f32),
+            pltpu.VMEM((width // LANES, slot_rows // length * spread(length), LANES), f32),
             pltpu.VMEM((ring_y, peers * length, width), bf16),
             pltpu.VMEM((ring_z, rows, width), bf16),
             pltpu.VMEM((ring_y, peers * length, width), bf16),
@@ -631,8 +648,13 @@
         ),
         name="return_gradients",
     )(
-        slot_total.reshape(ring_y, peers * length, width),
-        pool_total.reshape(ring_z, rows, width),
+        firsts,
+        places,
+        firsts,
+        places,
+        pool.reshape(pool_rows // length, length, width),
+        received.reshape(slot_rows // length, length, width),
+        laid,
         pick_rows,
         feature,
     )

time: 69.7 us -> 66.7 us (0.957)
  Pallas kernels: 68.7 us -> 65.7 us
    pallas_call x1 -> x0, Pallas kernels: 6.78 us -> none  [local(): pl.pallas_call(functools.partial(pair_kernel, length), out_shape=(shape((...]
    pallas_call x1, Pallas kernels: 22.9 us -> 26.7 us  [local(): pl.pallas_call(functools.partial(return_kernel, *layout), out_shape=shape...]
where the time goes in v3:
time: 66.7 us; the launch traced here: 66.6 us
  Pallas kernels  65.7 us (99%)
  matrix products  0.83 us (1%)
    pallas_call x1, Pallas kernels, local(): pl.pallas_call(functools.partial(gather_kernel, *layout), out_shape=(shap...  39 us
    pallas_call x1, Pallas kernels, local(): pl.pallas_call(functools.partial(return_kernel, *layout), out_shape=shape...  26.7 us

profile of v3, /device:TPU:1, one launch (start us, length us, event | category | flops | bytes accessed | tf_op | source)
XLA Modules:
  0.0 66.6 jit_solution(10867761299114400279)
XLA Ops:
  0.0 39.0 %gather_images.1 = (bf16[12,128,256]{2,1,0:T(8,128)(2,1)S(1)}, bf16[8,256,256]{2,1,0:T(8,128)(2,1)S(1)}, f32[1280,128]{1,0:T(8,128)S(1)}, s32[1,128]{1,0:T(1,128...) custom-call(s32[64]{0:T(128)} %picks_arg.1, bf16[128,256]{1,0:T(8,128)(2,1)} %bitcast.10, ...), custom_call_target="tpu_custom_call" | custom-call | tf_op jit(solution)/shard_map/gather_images/pallas_call | solution.py:584
  39.0 0.0 copy-start
  39.0 26.7 %return_gradients.1 = bf16[128,256]{1,0:T(8,128)(2,1)S(1)} custom-call(s32[1,128]{1,0:T(1,128)S(1)} %get-tuple-element.12.first_ref.firsts, s32[1,128]{1,0:T(1,128)S(1)} %get-tuple-element.13.place_ref.places, s32[1,128]{1,0:T(1,128)S(1)} %get-tuple-element.12.first_ref.firsts, s32[1,128]{1,0:T(1,128)S(1)} %get-tuple-element.13.place_ref.places, ...), custom_call_target="tpu_custom_call" | custom-call | tf_op jit(solution)/shard_map/return_gradients/pallas_call | solution.py:626
  65.7 0.0 copy-done
  65.7 0.8 %convolution_convert_fusion = bf16[128,256]{1,0:T(8,128)(2,1)} fusion(bf16[128,256]{1,0:T(8,128)(2,1)S(1)} %return_gradients.1, bf16[256,256]{1,0:T(8,128)(2,1)S(1)} %copy-done), kind=kOutput, calls=%fused_computation | convolution fusion | flops 16809984 | bytes 262144 | tf_op jit(solution)/shard_map/dot_general | solution.py:661
Async XLA Ops:
  39.0 26.7 %copy-start = (bf16[256,256]{1,0:T(8,128)(2,1)S(1)}, bf16[256,256]{1,0:T(8,128)(2,1)}, u32[]{:S(2)}) copy-start(bf16[256,256]{1,0:T(8,128)(2,1)} %weight_arg.1) | copy-start | bytes 393220

commit v4 on v3

--- a/solution.py
+++ b/solution.py
@@ -13,8 +13,9 @@
 LANES = 128
 VMEM_LIMIT = 40 * 1024 * 1024
 GRID = (4, 8, 2)
-STEPS_Y = {1: 0, 2: 0, 3: 2, 4: 2}
+STEPS_Y = {1: 0, 2: 0, 3: 1, 4: 2}
 STEPS_Z = {2: 0, 1: 0, 4: 2, 3: 2, 6: 4, 5: 4}
+ARRIVALS = "y1 z2 y2 z1 z4 y3 y4 z3 z6 z5"
 
 
 def place_of(offset, ring):
@@ -264,19 +265,19 @@
 
     tiles = grads.shape[1] // LANES
     todo = list(range(tiles))
-    for distance in range(1, max(half_y, half_z) + 1):
+    for arrival in ARRIVALS.split():
+        axis, distance = arrival[0], int(arrival[1:])
         if todo:
             lay(todo.pop(0))
-        if distance <= half_y:
+        if axis == "y" and distance <= half_y:
             for way in range(2):
                 y_copies[distance, way].wait_recv()
             forward_y(distance)
-        if distance <= half_z:
+            choose(distance, *plan[distance])
+        if axis == "z" and distance <= half_z:
             for way in range(2):
                 z_copies[distance, way].wait_recv()
             forward_z(distance)
-        if distance <= half_y:
-            choose(distance, *plan[distance])
     for tile in todo:
         lay(tile)
     for copy in x_copies:
@@ -291,7 +292,7 @@
     groups = pairs // across
     width = pool.shape[2]
     scale = 1.0 / (width * SOFTMAX_COOLING)
-    together = min(8, groups)
+    together = groups
 
     side = (LANES, LANES)
     row_block = lax.div(lax.broadcasted_iota(jnp.int32, side, 0), length)
@@ -434,7 +435,7 @@
     pair_gradients(
         length, first_ref, place_ref, pool_images, received, laid, by_first, by_second
     )
-    add_up(length, firsts, by_first, pool_total, pool)
+    add_up(length, places, by_second, slot_total, slots)
     met()
 
     y_copies, z_copies, x_copies = {}, {}, {}
@@ -470,10 +471,6 @@
                 here.along_y(turn * hop),
             )
 
-    for distance in range(half_z, 0, -1):
-        if distance not in steps_z.values():
-            send_z(distance)
-    add_up(length, places, by_second, slot_total, slots)
     for distance in range(half_y, -1, -1):
         place, count = plan[distance]
         x_copies[distance] = [
@@ -486,6 +483,10 @@
             )
             for turn in range(1, peers)
         ]
+    add_up(length, firsts, by_first, pool_total, pool)
+    for distance in range(half_z, 0, -1):
+        if distance not in steps_z.values():
+            send_z(distance)
     for at in range(ring_y):
         arrived[at, own] = slots[at, own]
         choosers[at] = chooser(pick_rows[at, :1], images, length)

time: 66.7 us -> 61 us (0.915)
  Pallas kernels: 65.7 us -> 60 us
    pallas_call x1, Pallas kernels: 26.7 us -> 23.5 us  [local(): pl.pallas_call(functools.partial(return_kernel, *layout), out_shape=shape...]
    pallas_call x1, Pallas kernels: 39 us -> 36.5 us  [local(): pl.pallas_call(functools.partial(gather_kernel, *layout), out_shape=(shap...]
where the time goes in v4:
time: 61 us; the launch traced here: 60.9 us
  Pallas kernels  60 us (98%)
  matrix products  0.83 us (1%)
    pallas_call x1, Pallas kernels, local(): pl.pallas_call(functools.partial(gather_kernel, *layout), out_shape=(shap...  36.5 us
    pallas_call x1, Pallas kernels, local(): pl.pallas_call(functools.partial(return_kernel, *layout), out_shape=shape...  23.5 us

profile of v4, /device:TPU:1, one launch (start us, length us, event | category | flops | bytes accessed | tf_op | source)
XLA Modules:
  0.0 60.9 jit_solution(6869497471882405613)
XLA Ops:
  0.0 36.5 %gather_images.1 = (bf16[12,128,256]{2,1,0:T(8,128)(2,1)S(1)}, bf16[8,256,256]{2,1,0:T(8,128)(2,1)S(1)}, f32[1280,128]{1,0:T(8,128)S(1)}, s32[1,128]{1,0:T(1,128...) custom-call(s32[64]{0:T(128)} %picks_arg.1, bf16[128,256]{1,0:T(8,128)(2,1)} %bitcast.10, ...), custom_call_target="tpu_custom_call" | custom-call | tf_op jit(solution)/shard_map/gather_images/pallas_call | solution.py:585
  36.5 0.0 copy-start
  36.5 23.5 %return_gradients.1 = bf16[128,256]{1,0:T(8,128)(2,1)S(1)} custom-call(s32[1,128]{1,0:T(1,128)S(1)} %get-tuple-element.12.first_ref.firsts, s32[1,128]{1,0:T(1,128)S(1)} %get-tuple-element.13.place_ref.places, s32[1,128]{1,0:T(1,128)S(1)} %get-tuple-element.12.first_ref.firsts, s32[1,128]{1,0:T(1,128)S(1)} %get-tuple-element.13.place_ref.places, ...), custom_call_target="tpu_custom_call" | custom-call | tf_op jit(solution)/shard_map/return_gradients/pallas_call | solution.py:627
  60.0 0.0 copy-done
  60.0 0.8 %convolution_convert_fusion = bf16[128,256]{1,0:T(8,128)(2,1)} fusion(bf16[128,256]{1,0:T(8,128)(2,1)S(1)} %return_gradients.1, bf16[256,256]{1,0:T(8,128)(2,1)S(1)} %copy-done), kind=kOutput, calls=%fused_computation | convolution fusion | flops 16809984 | bytes 262144 | tf_op jit(solution)/shard_map/dot_general | solution.py:662
Async XLA Ops:
  36.5 23.5 %copy-start = (bf16[256,256]{1,0:T(8,128)(2,1)S(1)}, bf16[256,256]{1,0:T(8,128)(2,1)}, u32[]{:S(2)}) copy-start(bf16[256,256]{1,0:T(8,128)(2,1)} %weight_arg.1) | copy-start | bytes 393220

commit v5 on v4

--- a/solution.py
+++ b/solution.py
@@ -15,7 +15,18 @@
 GRID = (4, 8, 2)
 STEPS_Y = {1: 0, 2: 0, 3: 1, 4: 2}
 STEPS_Z = {2: 0, 1: 0, 4: 2, 3: 2, 6: 4, 5: 4}
-ARRIVALS = "y1 z2 y2 z1 z4 y3 y4 z3 z6 z5"
+ARRIVALS = (
+    ("y", 1),
+    ("z", 2),
+    ("y", 2),
+    ("z", 1),
+    ("z", 4),
+    ("y", 3),
+    ("y", 4),
+    ("z", 3),
+    ("z", 6),
+    ("z", 5),
+)
 
 
 def place_of(offset, ring):
@@ -98,27 +109,24 @@
     return jnp.where(same & (image == pick_row), 1.0, 0.0).astype(jnp.bfloat16)
 
 
-def gather_kernel(
-    grid,
-    ring_z,
+def gather(
+    here,
     steps_y,
     steps_z,
     images,
     length,
-    picks_arg,
-    tokens_arg,
-    weight_arg,
-    grads_arg,
-    firsts_arg,
-    seconds_arg,
+    arguments,
     pool,
     received,
     laid,
+    first_ref,
     firsts,
+    place_ref,
     places,
     pick_rows,
     feature,
     picks,
+    second_ref,
     tokens,
     weight,
     grads,
@@ -133,10 +141,10 @@
     x_send,
     x_recv,
 ):
-    here = Where(grid, ring_z)
-    ring_y, peers = here.ring_y, here.peers
+    ring_y, ring_z, peers = here.ring_y, here.ring_z, here.peers
     rows, width = tokens.shape
     block_rows = blocks.shape[1]
+    picks_arg, tokens_arg, weight_arg, grads_arg, firsts_arg, seconds_arg = arguments
     fetches = [
         pltpu.make_async_copy(src, dst, fetch_sem.at[n])
         for n, (src, dst) in enumerate(
@@ -145,7 +153,9 @@
                 (weight_arg, weight),
                 (picks_arg, picks),
                 (seconds_arg, seconds),
+                (seconds_arg, second_ref),
                 (firsts_arg, firsts),
+                (firsts_arg, first_ref),
                 (grads_arg, grads),
             )
         )
@@ -161,7 +171,8 @@
     mean_square = jnp.mean(projected * projected, axis=-1, keepdims=True)
     normed = (projected * lax.rsqrt(mean_square + EPSILON)).astype(jnp.bfloat16)
     blocks[0, :rows] = normed
-    pool[here.z] = normed
+    for n in range(images):
+        pool[here.z * images + n] = normed[n * length : (n + 1) * length]
     tail = (block_rows - rows, peers * length)
     tail_row = lax.broadcasted_iota(jnp.int32, tail, 0)
     tail_peer = lax.div(lax.broadcasted_iota(jnp.int32, tail, 1), length)
@@ -197,11 +208,13 @@
             if before != source:
                 continue
             for way, turn in enumerate((1, -1)):
-                part = pl.ds(way * (rows // 2), rows // 2) if distance == half_z else pl.ds(0, rows)
-                owner = here.z_at(-turn * before)
+                first = here.z_at(-turn * before) * images
+                part = pl.ds(first, images)
+                if distance == half_z:
+                    part = pl.ds(first + way * (images // 2), images // 2)
                 z_copies[distance, way] = send(
-                    pool.at[owner, part],
-                    pool.at[owner, part],
+                    pool.at[part],
+                    pool.at[part],
                     z_send.at[way, distance - 1],
                     z_recv.at[way, distance - 1],
                     here.along_z(turn * (distance - before)),
@@ -224,14 +237,14 @@
             x_copies.append(
                 send(
                     stage.at[pl.ds(place, count), rows_at(here.s_at(turn), length)],
-                    received.at[pl.ds(place, count), own],
+                    received.at[pl.ds(place, count), here.s],
                     x_send.at[batch, turn - 1],
                     x_recv.at[batch, turn - 1],
                     here.across(turn),
                 )
             )
         for at in range(place, place + count):
-            received[at, own] = stage[at, own]
+            received[at, here.s] = stage[at, own]
 
     forward_y(0)
     forward_z(0)
@@ -240,12 +253,20 @@
     for fetch in fetches[3:]:
         fetch.wait()
 
-    slot = seconds[...]
-    offset = lax.rem(lax.rem(lax.div(slot, here.cores), ring_y) - here.y + ring_y, ring_y)
-    near = jnp.where(2 * offset <= ring_y, 2 * offset - 1, 2 * (ring_y - offset))
-    place = jnp.where(offset == 0, 0, near)
-    peer = lax.div(slot, here.cores * ring_y) * here.cores + lax.rem(slot, here.cores)
+    def find(slot):
+        offset = lax.rem(lax.rem(lax.div(slot, here.cores), ring_y) - here.y + ring_y, ring_y)
+        near = jnp.where(2 * offset <= ring_y, 2 * offset - 1, 2 * (ring_y - offset))
+        peer = lax.div(slot, here.cores * ring_y) * here.cores + lax.rem(slot, here.cores)
+        return jnp.where(offset == 0, 0, near), peer
+
+    place, peer = find(seconds[...])
     places[...] = place * peers + peer
+
+    def note(e, carry):
+        place_ref[0, e], place_ref[1, e] = find(second_ref[0, e])
+        return carry
+
+    lax.fori_loop(0, second_ref.shape[1], note, 0)
 
     across = LANES // length
     groups = grads.shape[0] // across
@@ -265,8 +286,7 @@
 
     tiles = grads.shape[1] // LANES
     todo = list(range(tiles))
-    for arrival in ARRIVALS.split():
-        axis, distance = arrival[0], int(arrival[1:])
+    for axis, distance in ARRIVALS:
         if todo:
             lay(todo.pop(0))
         if axis == "y" and distance <= half_y:
@@ -315,7 +335,11 @@
             g = chunk * together + n
             pairs_of_g = [q * groups + g for q in range(across)]
             firsts.append(jnp.concatenate([pool[first_ref[0, e]] for e in pairs_of_g], axis=0))
-            seconds.append(jnp.concatenate([received[place_ref[0, e]] for e in pairs_of_g], axis=0))
+            seconds.append(
+                jnp.concatenate(
+                    [received[place_ref[0, e], place_ref[1, e]] for e in pairs_of_g], axis=0
+                )
+            )
             full = lax.dot_general(
                 firsts[n],
                 seconds[n],
@@ -389,29 +413,17 @@
             ].astype(jnp.bfloat16)
 
 
-def return_kernel(
-    grid,
-    ring_z,
+def give_back(
+    here,
     steps_y,
     steps_z,
     images,
     length,
-    first_ref,
-    place_ref,
-    firsts,
-    places,
-    pool_images,
-    received,
-    laid,
+    sum_pool,
+    slots,
+    pool,
     pick_rows,
     feature,
-    feature_grad,
-    by_first,
-    by_second,
-    pool_total,
-    slot_total,
-    slots,
-    pool,
     arrived,
     choosers,
     y_in,
@@ -425,19 +437,11 @@
     x_send,
     x_recv,
 ):
-    here = Where(grid, ring_z)
-    ring_y, peers = here.ring_y, here.peers
+    ring_y, ring_z, peers = here.ring_y, here.ring_z, here.peers
     rows, width = feature.shape
     half_y, half_z = ring_y // 2, ring_z // 2
-    met = here.greet(steps_y, steps_z)
     own = rows_at(here.s, length)
     plan = batches(ring_y)
-    pair_gradients(
-        length, first_ref, place_ref, pool_images, received, laid, by_first, by_second
-    )
-    add_up(length, places, by_second, slot_total, slots)
-    met()
-
     y_copies, z_copies, x_copies = {}, {}, {}
 
     def part_of(distance, way, half):
@@ -483,7 +487,7 @@
             )
             for turn in range(1, peers)
         ]
-    add_up(length, firsts, by_first, pool_total, pool)
+    sum_pool()
     for distance in range(half_z, 0, -1):
         if distance not in steps_z.values():
             send_z(distance)
@@ -541,17 +545,31 @@
         gradient = collect(gradient, way, 0, *along_z)
         gradient = collect(gradient, way, 0, *along_y)
     mean = jnp.mean(gradient * normed, axis=-1, keepdims=True)
-    feature_grad[...] = (inv_rms * (gradient - normed * mean)).astype(jnp.bfloat16)
     for copy in [*y_copies.values(), *z_copies.values(), *sum(x_copies.values(), [])]:
         copy.wait_send()
-
-
-def in_vmem(count):
-    return [pl.BlockSpec(memory_space=pltpu.VMEM)] * count
-
-
-def in_smem(count):
-    return [pl.BlockSpec(memory_space=pltpu.SMEM)] * count
+    return (inv_rms * (gradient - normed * mean)).astype(jnp.bfloat16)
+
+
+def kernel(grid, ring_z, steps_y, steps_z, images, length, *refs):
+    arguments, (feature_grad, *scratch) = refs[:6], refs[6:]
+    gathered, fetched, moved, sems = scratch[:9], scratch[9:17], scratch[17:29], scratch[29:]
+    pool_images, received, laid, first_ref, firsts, place_ref, places, pick_rows, feature = gathered
+    by_first, by_second, pool_total, slot_total, slots, pool, *rings = moved
+    here = Where(grid, ring_z)
+    common = (here, steps_y, steps_z, images, length)
+    gather(*common, arguments, *gathered, *fetched, *sems[:7])
+    pair_gradients(length, first_ref, place_ref, pool_images, received, laid, by_first, by_second)
+    add_up(length, places, by_second, slot_total, slots)
+    feature_grad[...] = give_back(
+        *common,
+        lambda: add_up(length, firsts, by_first, pool_total, pool),
+        slots,
+        pool,
+        pick_rows,
+        feature,
+        *rings,
+        *sems[7:],
+    )
 
 
 def ring_semaphores(half_y, half_z, peers):
@@ -579,37 +597,51 @@
     half_y, half_z = ring_y // 2, ring_z // 2
     layout = (grid, ring_z, steps_y, steps_z, images, length)
     bf16, f32 = jnp.bfloat16, jnp.float32
-    shape = jax.ShapeDtypeStruct
-    pool_rows, slot_rows = ring_z * rows, ring_y * peers * length
-
-    pool, received, laid, firsts, places, pick_rows, feature = pl.pallas_call(
-        functools.partial(gather_kernel, *layout),
-        out_shape=(
-            shape((ring_z, rows, width), bf16),
-            shape((ring_y, peers * length, width), bf16),
-            shape((length * spread(pairs * length // LANES), LANES), f32),
-            shape((1, pairs), jnp.int32),
-            shape((1, pairs), jnp.int32),
-            shape((ring_y, 8, peers * length), f32),
-            shape((rows, width), f32),
-        ),
+
+    block = (ring_y, peers * length, width)
+    feature_grad = pl.pallas_call(
+        functools.partial(kernel, *layout),
+        out_shape=jax.ShapeDtypeStruct((rows, width), bf16),
         in_specs=[pl.BlockSpec(memory_space=pltpu.HBM)] * 6,
-        out_specs=tuple(in_vmem(7)),
+        out_specs=pl.BlockSpec(memory_space=pltpu.VMEM),
         scratch_shapes=[
+            pltpu.VMEM((ring_z * images, length, width), bf16),
+            pltpu.VMEM((ring_y, peers, length, width), bf16),
+            pltpu.VMEM((length * spread(pairs * length // LANES), LANES), f32),
+            pltpu.SMEM((1, pairs), jnp.int32),
+            pltpu.VMEM((1, pairs), jnp.int32),
+            pltpu.SMEM((2, pairs), jnp.int32),
+            pltpu.VMEM((1, pairs), jnp.int32),
+            pltpu.VMEM((ring_y, 8, peers * length), f32),
+            pltpu.VMEM((rows, width), f32),
             pltpu.SMEM((send_pick.shape[0],), jnp.int32),
+            pltpu.SMEM((1, pairs), jnp.int32),
             pltpu.VMEM((rows, width), bf16),
             pltpu.VMEM(proj_weight.shape, bf16),
             pltpu.VMEM(match_grad.shape, bf16),
             pltpu.VMEM((1, pairs), jnp.int32),
             pltpu.VMEM((ring_y, rows + 16, width), bf16),
-            pltpu.VMEM((ring_y, peers * length, width), bf16),
-            pltpu.SemaphoreType.DMA((6,)),
+            pltpu.VMEM(block, bf16),
+            pltpu.VMEM((width // LANES, length * spread(pairs), LANES), f32),
+            pltpu.VMEM((width // LANES, length * spread(pairs), LANES), f32),
+            pltpu.VMEM((width // LANES, ring_z * images * spread(length), LANES), f32),
+            pltpu.VMEM((width // LANES, ring_y * peers * spread(length), LANES), f32),
+            pltpu.VMEM(block, bf16),
+            pltpu.VMEM((ring_z, rows, width), bf16),
+            pltpu.VMEM(block, bf16),
+            pltpu.VMEM((ring_y, rows, peers * length), bf16),
+            pltpu.VMEM((2, half_y, rows, width), bf16),
+            pltpu.VMEM((2, half_y, rows, width), bf16),
+            pltpu.VMEM((2, half_z, rows, width), bf16),
+            pltpu.VMEM((2, half_z, rows, width), bf16),
+            pltpu.SemaphoreType.DMA((8,)),
+            *ring_semaphores(half_y, half_z, peers),
             *ring_semaphores(half_y, half_z, peers),
         ],
         compiler_params=pltpu.CompilerParams(
             collective_id=0, has_side_effects=True, vmem_limit_bytes=VMEM_LIMIT
         ),
-        name="gather_images",
+        name="feature_gradients",
     )(
         *(
             pltpu.with_memory_space_constraint(argument, pltpu.HBM)
@@ -622,42 +654,6 @@
                 pair_second_image.reshape(1, pairs),
             )
         )
-    )
-
-    feature_grad = pl.pallas_call(
-        functools.partial(return_kernel, *layout),
-        out_shape=shape((rows, width), bf16),
-        in_specs=in_smem(2) + in_vmem(7),
-        out_specs=pl.BlockSpec(memory_space=pltpu.VMEM),
-        scratch_shapes=[
-            pltpu.VMEM((width // LANES, length * spread(pairs), LANES), f32),
-            pltpu.VMEM((width // LANES, length * spread(pairs), LANES), f32),
-            pltpu.VMEM((width // LANES, pool_rows // length * spread(length), LANES), f32),
-            pltpu.VMEM((width // LANES, slot_rows // length * spread(length), LANES), f32),
-            pltpu.VMEM((ring_y, peers * length, width), bf16),
-            pltpu.VMEM((ring_z, rows, width), bf16),
-            pltpu.VMEM((ring_y, peers * length, width), bf16),
-            pltpu.VMEM((ring_y, rows, peers * length), bf16),
-            pltpu.VMEM((2, half_y, rows, width), bf16),
-            pltpu.VMEM((2, half_y, rows, width), bf16),
-            pltpu.VMEM((2, half_z, rows, width), bf16),
-            pltpu.VMEM((2, half_z, rows, width), bf16),
-            *ring_semaphores(half_y, half_z, peers),
-        ],
-        compiler_params=pltpu.CompilerParams(
-            collective_id=1, has_side_effects=True, vmem_limit_bytes=VMEM_LIMIT
-        ),
-        name="return_gradients",
-    )(
-        firsts,
-        places,
-        firsts,
-        places,
-        pool.reshape(pool_rows // length, length, width),
-        received.reshape(slot_rows // length, length, width),
-        laid,
-        pick_rows,
-        feature,
     )
     token_grad = lax.dot_general(
         feature_grad, proj_weight, (((1,), (1,)), ((), ())), preferred_element_type=f32

time: 61 us -> 59.5 us (0.975)
  Pallas kernels: 60 us -> 58.5 us
    pallas_call x2 -> x1, Pallas kernels: 60 us -> 58.5 us  [local(): pl.pallas_call(functools.partial(kernel, *layout), out_shape=jax.ShapeDty...]
where the time goes in v5:
time: 59.5 us; the launch traced here: 59.3 us
  Pallas kernels  58.5 us (98%)
  matrix products  0.83 us (1%)
    pallas_call x1, Pallas kernels, local(): pl.pallas_call(functools.partial(kernel, *layout), out_shape=jax.ShapeDty...  58.5 us

profile of v5, /device:TPU:1, one launch (start us, length us, event | category | flops | bytes accessed | tf_op | source)
XLA Modules:
  0.0 59.3 jit_solution(9706952598315126307)
XLA Ops:
  0.0 0.0 copy-start
  0.0 58.5 %feature_gradients.1 = bf16[128,256]{1,0:T(8,128)(2,1)S(1)} custom-call(s32[64]{0:T(128)} %refs_0_.1, bf16[128,256]{1,0:T(8,128)(2,1)} %bitcast.6, bf16[256,256]{1,0:T(8,128)(2,1)} %refs_2_.1, bf16[128,1024]{1,0:T(8,128)(2,1)} %refs_3_.1, s32[1,128]{1,0:T(1,128)} %bitcast.7, s32[1,128]{1,0:T(1,128)} %bitcast.8), custom_call_target="tpu_custom_call" | custom-call | tf_op jit(solution)/shard_map/feature_gradients/pallas_call | solution.py:602
  58.5 0.0 copy-done
  58.5 0.8 %convolution_convert_fusion = bf16[128,256]{1,0:T(8,128)(2,1)} fusion(bf16[128,256]{1,0:T(8,128)(2,1)S(1)} %feature_gradients.1, bf16[256,256]{1,0:T(8,128)(2,1)S(1)} %copy-done), kind=kOutput, calls=%fused_computation | convolution fusion | flops 16809984 | bytes 262144 | tf_op jit(solution)/shard_map/dot_general | solution.py:658
Async XLA Ops:
  0.0 58.5 %copy-start = (bf16[256,256]{1,0:T(8,128)(2,1)S(1)}, bf16[256,256]{1,0:T(8,128)(2,1)}, u32[]{:S(2)}) copy-start(bf16[256,256]{1,0:T(8,128)(2,1)} %refs_2_.1) | copy-start | bytes 393220

commit v6 on v5

--- a/solution.py
+++ b/solution.py
@@ -145,6 +145,7 @@
     rows, width = tokens.shape
     block_rows = blocks.shape[1]
     picks_arg, tokens_arg, weight_arg, grads_arg, firsts_arg, seconds_arg = arguments
+    met = here.greet(steps_y, steps_z)
     fetches = [
         pltpu.make_async_copy(src, dst, fetch_sem.at[n])
         for n, (src, dst) in enumerate(
@@ -162,8 +163,6 @@
     ]
     for fetch in fetches:
         fetch.start()
-    met = here.greet(steps_y, steps_z)
-
     for fetch in fetches[:3]:
         fetch.wait()
     projected = jnp.dot(tokens[...], weight[...], preferred_element_type=jnp.float32)
@@ -306,7 +305,37 @@
         copy.wait_send()
 
 
-def pair_gradients(length, first_ref, place_ref, pool, received, laid, by_first, by_second):
+def put_rows(by_pair, pair, length, pairs, values):
+    for h in range(by_pair.shape[0]):
+        by_pair[h, pl.ds(pair, length, stride=spread(pairs)), :] = values[
+            :, h * LANES : (h + 1) * LANES
+        ]
+
+
+def on_diagonal(packed, length):
+    side = (LANES, LANES)
+    row_block = lax.div(lax.broadcasted_iota(jnp.int32, side, 0), length)
+    lane_block = lax.div(lax.broadcasted_iota(jnp.int32, side, 1), length)
+    wide = jnp.concatenate([packed] * (LANES // length), axis=0)
+    return jnp.where(row_block == lane_block, wide, jnp.zeros_like(wide))
+
+
+def first_gradients(length, place_ref, received, d_scores, by_first):
+    pairs = place_ref.shape[1]
+    across = LANES // length
+    groups = pairs // across
+    for g in range(groups):
+        pairs_of_g = [q * groups + g for q in range(across)]
+        second = jnp.concatenate(
+            [received[place_ref[0, e], place_ref[1, e]] for e in pairs_of_g], axis=0
+        )
+        wide = on_diagonal(d_scores[g * length : (g + 1) * length], length)
+        grad_first = jnp.dot(wide, second, preferred_element_type=jnp.float32)
+        for q, e in enumerate(pairs_of_g):
+            put_rows(by_first, e, length, pairs, grad_first[q * length : (q + 1) * length])
+
+
+def pair_gradients(length, first_ref, place_ref, pool, received, laid, d_scores, by_second):
     pairs = first_ref.shape[1]
     across = LANES // length
     groups = pairs // across
@@ -362,21 +391,17 @@
         over_first = jnp.sum(both.reshape(shape), axis=1, keepdims=True)
         part = (cols.reshape(shape) * over_first).reshape(rows.shape)
         d_scaled = ((2.0 * both - rows * over_second - part) * scale).astype(jnp.bfloat16)
+        at = pl.multiple_of(chunk * (together * length), together * length)
+        d_scores[pl.ds(at, together * length)] = d_scaled
         for n in range(together):
-            mine = d_scaled[n * length : (n + 1) * length]
-            wide = jnp.concatenate([mine] * across, axis=0)
-            wide = jnp.where(diagonal, wide, jnp.zeros_like(wide))
-            grad_first = jnp.dot(wide, seconds[n], preferred_element_type=jnp.float32)
+            wide = on_diagonal(d_scaled[n * length : (n + 1) * length], length)
             grad_second = lax.dot_general(
                 wide, firsts[n], (((0,), (0,)), ((), ())), preferred_element_type=jnp.float32
             )
             for q in range(across):
                 part = slice(q * length, (q + 1) * length)
-                rows_of_pair = pl.ds(q * groups + chunk * together + n, length, stride=spread(pairs))
-                for h in range(width // LANES):
-                    lanes = slice(h * LANES, (h + 1) * LANES)
-                    by_first[h, rows_of_pair, :] = grad_first[part, lanes]
-                    by_second[h, rows_of_pair, :] = grad_second[part, lanes]
+                pair = q * groups + chunk * together + n
+                put_rows(by_second, pair, length, pairs, grad_second[part])
         return carry
 
     lax.fori_loop(0, groups // together, step, 0)
@@ -552,17 +577,22 @@
 
 def kernel(grid, ring_z, steps_y, steps_z, images, length, *refs):
     arguments, (feature_grad, *scratch) = refs[:6], refs[6:]
-    gathered, fetched, moved, sems = scratch[:9], scratch[9:17], scratch[17:29], scratch[29:]
+    gathered, fetched, moved, sems = scratch[:9], scratch[9:17], scratch[17:30], scratch[30:]
     pool_images, received, laid, first_ref, firsts, place_ref, places, pick_rows, feature = gathered
-    by_first, by_second, pool_total, slot_total, slots, pool, *rings = moved
+    d_scores, by_first, by_second, pool_total, slot_total, slots, pool, *rings = moved
     here = Where(grid, ring_z)
     common = (here, steps_y, steps_z, images, length)
     gather(*common, arguments, *gathered, *fetched, *sems[:7])
-    pair_gradients(length, first_ref, place_ref, pool_images, received, laid, by_first, by_second)
+    pair_gradients(length, first_ref, place_ref, pool_images, received, laid, d_scores, by_second)
     add_up(length, places, by_second, slot_total, slots)
+
+    def sum_pool():
+        first_gradients(length, place_ref, received, d_scores, by_first)
+        add_up(length, firsts, by_first, pool_total, pool)
+
     feature_grad[...] = give_back(
         *common,
-        lambda: add_up(length, firsts, by_first, pool_total, pool),
+        sum_pool,
         slots,
         pool,
         pick_rows,
@@ -622,6 +652,7 @@
             pltpu.VMEM((1, pairs), jnp.int32),
             pltpu.VMEM((ring_y, rows + 16, width), bf16),
             pltpu.VMEM(block, bf16),
+            pltpu.VMEM((pairs * length * length // LANES, LANES), bf16),
             pltpu.VMEM((width // LANES, length * spread(pairs), LANES), f32),
             pltpu.VMEM((width // LANES, length * spread(pairs), LANES), f32),
             pltpu.VMEM((width // LANES, ring_z * images * spread(length), LANES), f32),

time: 59.5 us -> 58.8 us (0.988)
  Pallas kernels: 58.5 us -> 57.6 us
    pallas_call x1, Pallas kernels: 58.5 us -> 57.6 us  [local(): pl.pallas_call(functools.partial(kernel, *layout), out_shape=jax.ShapeDty...]
where the time goes in v6:
time: 58.8 us; the launch traced here: 58.4 us
  Pallas kernels  57.6 us (98%)
  matrix products  0.83 us (1%)
    pallas_call x1, Pallas kernels, local(): pl.pallas_call(functools.partial(kernel, *layout), out_shape=jax.ShapeDty...  57.6 us

profile of v6, /device:TPU:1, one launch (start us, length us, event | category | flops | bytes accessed | tf_op | source)
XLA Modules:
  0.0 58.4 jit_solution(10354079201159040358)
XLA Ops:
  0.0 0.0 copy-start
  0.0 57.6 %feature_gradients.1 = bf16[128,256]{1,0:T(8,128)(2,1)S(1)} custom-call(s32[64]{0:T(128)} %refs_0_.1, bf16[128,256]{1,0:T(8,128)(2,1)} %bitcast.6, bf16[256,256]{1,0:T(8,128)(2,1)} %refs_2_.1, bf16[128,1024]{1,0:T(8,128)(2,1)} %refs_3_.1, s32[1,128]{1,0:T(1,128)} %bitcast.7, s32[1,128]{1,0:T(1,128)} %bitcast.8), custom_call_target="tpu_custom_call" | custom-call | tf_op jit(solution)/shard_map/feature_gradients/pallas_call | solution.py:632
  57.6 0.0 copy-done
  57.6 0.8 %convolution_convert_fusion = bf16[128,256]{1,0:T(8,128)(2,1)} fusion(bf16[128,256]{1,0:T(8,128)(2,1)S(1)} %feature_gradients.1, bf16[256,256]{1,0:T(8,128)(2,1)S(1)} %copy-done), kind=kOutput, calls=%fused_computation | convolution fusion | flops 16809984 | bytes 262144 | tf_op jit(solution)/shard_map/dot_general | solution.py:689
Async XLA Ops:
  0.0 57.6 %copy-start = (bf16[256,256]{1,0:T(8,128)(2,1)S(1)}, bf16[256,256]{1,0:T(8,128)(2,1)}, u32[]{:S(2)}) copy-start(bf16[256,256]{1,0:T(8,128)(2,1)} %refs_2_.1) | copy-start | bytes 393220

commit v7 on v6

--- a/solution.py
+++ b/solution.py
@@ -258,14 +258,14 @@
         peer = lax.div(slot, here.cores * ring_y) * here.cores + lax.rem(slot, here.cores)
         return jnp.where(offset == 0, 0, near), peer
 
-    place, peer = find(seconds[...])
-    places[...] = place * peers + peer
-
     def note(e, carry):
         place_ref[0, e], place_ref[1, e] = find(second_ref[0, e])
         return carry
 
-    lax.fori_loop(0, second_ref.shape[1], note, 0)
+    def find_all():
+        place, peer = find(seconds[...])
+        places[...] = place * peers + peer
+        lax.fori_loop(0, second_ref.shape[1], note, 0)
 
     across = LANES // length
     groups = grads.shape[0] // across
@@ -293,6 +293,8 @@
                 y_copies[distance, way].wait_recv()
             forward_y(distance)
             choose(distance, *plan[distance])
+            if distance == half_y:
+                find_all()
         if axis == "z" and distance <= half_z:
             for way in range(2):
                 z_copies[distance, way].wait_recv()

time: 58.8 us -> 58.7 us (level)
  no operation moved by 1% of the time
where the time goes in v7:
time: 58.7 us; the launch traced here: 58.4 us
  Pallas kernels  57.6 us (98%)
  matrix products  0.84 us (1%)
    pallas_call x1, Pallas kernels, local(): pl.pallas_call(functools.partial(kernel, *layout), out_shape=jax.ShapeDty...  57.6 us

profile of v7, /device:TPU:1, one launch (start us, length us, event | category | flops | bytes accessed | tf_op | source)
XLA Modules:
  0.0 58.4 jit_solution(6516063328037626636)
XLA Ops:
  0.0 0.0 copy-start
  0.0 57.6 %feature_gradients.1 = bf16[128,256]{1,0:T(8,128)(2,1)S(1)} custom-call(s32[64]{0:T(128)} %refs_0_.1, bf16[128,256]{1,0:T(8,128)(2,1)} %bitcast.6, bf16[256,256]{1,0:T(8,128)(2,1)} %refs_2_.1, bf16[128,1024]{1,0:T(8,128)(2,1)} %refs_3_.1, s32[1,128]{1,0:T(1,128)} %bitcast.7, s32[1,128]{1,0:T(1,128)} %bitcast.8), custom_call_target="tpu_custom_call" | custom-call | tf_op jit(solution)/shard_map/feature_gradients/pallas_call | solution.py:634
  57.6 0.0 copy-done
  57.6 0.8 %convolution_convert_fusion = bf16[128,256]{1,0:T(8,128)(2,1)} fusion(bf16[128,256]{1,0:T(8,128)(2,1)S(1)} %feature_gradients.1, bf16[256,256]{1,0:T(8,128)(2,1)S(1)} %copy-done), kind=kOutput, calls=%fused_computation | convolution fusion | flops 16809984 | bytes 262144 | tf_op jit(solution)/shard_map/dot_general | solution.py:691
Async XLA Ops:
  0.0 57.6 %copy-start = (bf16[256,256]{1,0:T(8,128)(2,1)S(1)}, bf16[256,256]{1,0:T(8,128)(2,1)}, u32[]{:S(2)}) copy-start(bf16[256,256]{1,0:T(8,128)(2,1)} %refs_2_.1) | copy-start | bytes 393220
